TPU v7x, 32 devices: a whole 2x2x4 slice. The times are simulated.
32 devices in a mesh: dec: 8 (over z, core), tp: 4 (over y, x).
Axes of the slice: x: 2, y: 2, z: 4, core: 2. Of those that a mesh axis runs over, the one named last changes fastest.
Arguments:
- hidden: float32 [8, 8, 4, 4096], P('dec', 'tp'), may hold values from -500 to 500
- norm_gain: float32 [4096], replicated, may hold values from 0.5 to 1.5
- lm_head: bfloat16 [16384, 4096], P(('dec', 'tp')), may hold values from -1 to 1
- token_ids: int32 [8, 8, 4], P('dec'), may hold values from 0 to 16383
- doc_counts: int32 [8], P('dec'), may hold values from 2 to 8, as said below
Outputs:
- hyp_score: float32 [8, 8], P('dec', 'tp')
- posterior: float32 [8, 8], P('dec', 'tp')
Inputs may be any that keep to these rules, and one draw needn't show every extreme that they name: Document d's live hypotheses are its slots 0 to doc_counts[d] - 1; some document has 8.
All inputs are finite; a program needn't handle non-finite values.
Results may differ from a plain program's by a relative error of at most 0.0021.
Values may be sent and summed in bfloat16 or wider, within the bound.
A program may use at most 64 MiB of HBM per device.

v0:
```python
import jax
import jax.numpy as jnp
from jax import lax
from jax.sharding import PartitionSpec as P


def rms_normed(hidden, norm_gain):
    flat = hidden.reshape(-1, hidden.shape[-1])
    meansq = jnp.mean(flat * flat, axis=1, keepdims=True)
    return (flat * lax.rsqrt(meansq + 1e-05) * norm_gain).astype(jnp.bfloat16)


def body(hidden, norm_gain, lm_head, token_ids, doc_counts):
    tp_count = lax.axis_size("tp")
    tp_index = lax.axis_index("tp")
    dec_index = lax.axis_index("dec")
    slot_count = hidden.shape[1]
    length = hidden.shape[2]
    vocab_rows = lm_head.shape[0]
    normed = rms_normed(hidden, norm_gain)
    doc_ids = token_ids[0]
    vocab_start = (dec_index * tp_count + tp_index) * vocab_rows
    own_slots = tp_index * slot_count + jnp.arange(slot_count, dtype=jnp.int32)
    sent_ids = lax.dynamic_slice_in_dim(doc_ids, tp_index * slot_count, slot_count, 0).reshape(-1)
    group_rows, group_ids = (
        lax.all_gather(normed, "tp", axis=0, tiled=True),
        lax.all_gather(sent_ids, "tp", axis=0, tiled=True),
    )
    seg_rows = lax.all_gather(group_rows, "dec", axis=0, tiled=True)
    seg_ids = lax.all_gather(group_ids, "dec", axis=0, tiled=True)
    logits = lax.dot_general(
        seg_rows, lm_head, (((1,), (1,)), ((), ())), preferred_element_type=jnp.float32
    )
    peak_value = jnp.max(logits, axis=1)
    exp_total = jnp.sum(jnp.exp(logits - peak_value[:, None]), axis=1)
    local_ids = seg_ids - vocab_start
    matches = jnp.arange(vocab_rows, dtype=jnp.int32)[None, :] == local_ids[:, None]
    target = jnp.sum(jnp.where(matches, logits, 0.0), axis=1)
    fresh = (peak_value, exp_total, target)
    peak_value, exp_total, target = tuple((new for new in fresh))
    block_slot = jnp.arange(tp_count * slot_count, dtype=jnp.int32)
    block_rows = tp_count * slot_count * length
    global_peak = lax.pmax(peak_value, ("dec", "tp"))
    scaled = exp_total * jnp.exp(peak_value - global_peak)
    sum_exp, target_sum = lax.psum((scaled, target), ("dec", "tp"))
    token_logp = target_sum - (global_peak + jnp.log(sum_exp))
    doc_logp = lax.dynamic_slice_in_dim(token_logp, dec_index * block_rows, block_rows, 0)
    block_scores = jnp.sum(doc_logp.reshape(-1, length), axis=1) / length
    alive = block_slot < doc_counts[0]
    best_score = jnp.max(jnp.where(alive, block_scores, -jnp.inf))
    doc_norm = best_score + jnp.log(
        jnp.sum(jnp.exp(jnp.where(alive, block_scores - best_score, -jnp.inf)))
    )
    picked = jnp.take(block_scores, own_slots)
    own_alive = own_slots < doc_counts[0]
    hyp_score = jnp.where(own_alive, picked, 0.0)[None, :]
    posterior = jnp.where(own_alive, picked - doc_norm, 0.0)[None, :]
    return (hyp_score, posterior)


def solution(mesh):
    placed = (
        P("dec", "tp", None, None),
        P(),
        P(("dec", "tp"), None),
        P("dec", None, None),
        P("dec"),
    )
    return jax.shard_map(
        body,
        mesh=mesh,
        in_specs=placed,
        out_specs=(P("dec", "tp"), P("dec", "tp")),
        check_vma=False,
    )
```

profile of v0, /device:TPU:0, one launch (start us, length us, event | category | flops | bytes accessed | tf_op | source)
XLA Modules:
  0.0 146.2 jit_solution(17324789163802871874)
XLA Ops:
  7.2 0.0 copy-start
  7.2 0.0 all-gather.2.cloned.1.call-start
  7.2 1.0 reshape.106
  8.2 1.0 multiply_reduce_fusion
  9.2 0.1 rsqrt.12
  9.3 0.8 multiply_convert_fusion
  10.1 11.1 %all_gather.14 = bf16[32,4096]{1,0:T(8,128)(2,1)} all-gather(bf16[8,4096]{1,0:T(8,128)(2,1)S(1)} %multiply_convert_fusion), channel_id=1, replica_groups=mesh['dec'=8,'tp'=4] {'tp'}, dimensions={0}, use_global_device_ids=true | all-gather | bytes 327680 | tf_op jit(solution)/shard_map/all_gather | solution.py:26
  21.2 0.0 all-gather.2.cloned.1.call-update
  21.9 0.0 copy-done
  21.9 0.1 constant_dynamic-slice_fusion
  22.0 0.1 copy.8
  22.1 0.1 reshape.116
  22.2 1.2 dynamic-slice.1
  23.4 1.2 dynamic-slice.2
  26.0 0.2 dynamic-update-slice
  26.2 7.3 %all-reduce = s32[32]{0:T(128)S(1)} all-reduce(s32[32]{0:T(128)S(1)} %dynamic-update-slice), channel_id=1, replica_groups=mesh['dec'=8,'tp'=4] {'tp'}, use_global_device_ids=true, to_apply=%add | all-reduce | flops 32 | bytes 256
  33.5 0.2 dynamic-update-slice.1
  33.7 9.4 %all-reduce.1 = s32[256]{0:T(256)S(1)} all-reduce(s32[256]{0:T(256)S(1)} %dynamic-update-slice.1), channel_id=1, replica_groups=mesh['dec'=8,'tp'=4] {'dec'}, use_global_device_ids=true, to_apply=%add.1 | all-reduce | flops 256 | bytes 2048
  43.1 7.9 %all-gather.2.cloned.1.call-done = bf16[256,4096]{1,0:T(8,128)(2,1)} async-done(((bf16[32,4096]{1,0:T(8,128)(2,1)}), bf16[256,4096]{1,0:T(8,128)(2,1)}) %all-gather.2.cloned.1.call-update) | async-done | bytes 2097168 | tf_op jit(solution)/shard_map/all_gather | solution.py:29
  51.0 4.2 %fusion.4 = (f32[256]{0:T(256)S(1)}, f32[256,512]{1,0:T(8,128)S(1)}) fusion(bf16[256,4096]{1,0:T(8,128)(2,1)} %all-gather.2.cloned.1.call-done, bf16[512,4096]{1,0:T(8,128)(2,1)} %param.7), kind=kOutput, calls=%fused_computation.25 | convolution fusion | flops 1073872640 | bytes 6816768 | tf_op jit(solution)/shard_map/dot_general | solution.py:31
  55.2 40.2 %pmax.7 = f32[256]{0:T(256)S(1)} all-reduce(f32[256]{0:T(256)S(1)} %get-tuple-element.10), channel_id=1, replica_groups=mesh['dec'=8,'tp'=4] {'dec','tp'}, use_global_device_ids=true, to_apply=%region_4.5 | all-reduce | flops 256 | bytes 2048 | tf_op jit(solution)/shard_map/pmax | solution.py:43
  95.4 0.3 exponential_reduce_fusion
  95.7 39.0 %all-reduce.2 = (f32[256]{0:T(256)S(1)}, f32[256]{0:T(256)S(1)}) all-reduce(f32[256]{0:T(256)S(1)} %get-tuple-element.3, f32[256]{0:T(256)S(1)} %exponential_multiply_fusion), channel_id=1, replica_groups=mesh['dec'=8,'tp'=4] {'dec','tp'}, use_global_device_ids=true, to_apply=%region_2.0 | all-reduce | flops 512 | bytes 4096 | tf_op jit(solution)/shard_map/psum | solution.py:45
  134.7 0.1 dynamic_slice.7
  134.8 0.1 reshape.107
  134.9 0.1 reduce_sum.48
  135.0 0.6 fusion
  135.6 1.3 fusion.2
  138.2 0.6 gather_fusion
  138.8 0.5 compare_select_fusion.4
  (8 shorter events, 0.0 us)
Async XLA Ops:
  7.2 14.8 %copy-start = (s32[1,8,4]{1,2,0:T(4,128)S(1)}, s32[1,8,4]{1,2,0:T(4,128)}, u32[]{:S(2)}) copy-start(s32[1,8,4]{1,2,0:T(4,128)} %param.8) | copy-start | bytes 388
  7.2 43.8 %all-gather.2.cloned.1.call-start = ((), (), s32[]{:S(2)}) async-start(), calls=%async_computation | async-start | bytes 2359296 | tf_op jit(solution)/shard_map/all_gather | solution.py:29
Sparse Core Ops, SparseCore 0:
  21.4 29.5 all-gather.1
where the time goes:
time: 147 us; the launch traced here: 146 us
  blocking collectives  107 us (73%)
  between operations  17.4 us (12%)
  waiting for transfers between devices  7.88 us (5%)
  local copies, waits for them, and re-layouts  5 us (3%)
  other arithmetic  4.67 us (3%)
  matrix products  4.18 us (3%)
    pmax x1, blocking collectives, body(): global_peak = lax.pmax(peak_value, ('dec', 'tp'))  40.2 us
    psum x1, blocking collectives, body(): sum_exp, target_sum = lax.psum((scaled, target), ('dec', 'tp'))  39 us
    unnamed x2, blocking collectives  16.7 us
    all_gather x1, blocking collectives, body(): lax.all_gather(normed, 'tp', axis=0, tiled=True)  11.1 us
    all_gather x1, waiting for transfers between devices, body(): seg_rows = lax.all_gather(group_rows, 'dec', axis=0, tiled=True)  7.87 us
    dot_general x1, matrix products, body(): lax.dot_general(seg_rows, lm_head, (((1,), (1,)), ((), ())), preferred_el...  4.18 us
  transfers between devices with their start and end apart: 1, of which 1 were waited for; matrix products, arithmetic and copies ran while one was open for 2% of the time, Pallas kernels for 0%

commit v1 on v0

v1 whole, which is shorter than its diff:
```python
import functools

import jax
import jax.numpy as jnp
from jax import lax
from jax.experimental import pallas as pl
from jax.experimental.pallas import tpu as pltpu
from jax.sharding import PartitionSpec as P

MESH = pl.DeviceIdType.MESH
CORES = 2
HALVES = 2
EPS = 1e-05


def flip(index, mask):
    bit = 1
    while bit <= mask:
        if mask & bit:
            index = index + bit - 2 * bit * ((index // bit) % 2)
        bit *= 2
    return index


def kernel(dec_n, tp_n, hidden, gain, lm_head, ids, counts, hyp_ref, post_ref,
           weights, rows, doc_ids, id_row, fresh, logits, stat_row, stats, got_dec, stat_doc, got_tp,
           w_sem, send_sem, recv_sem, id_send, id_recv, dec_send, dec_recv, tp_send, tp_recv):
    slots, length, width = hidden.shape[1:]
    own_rows = slots * length
    doc_rows = tp_n * own_rows
    vocab = lm_head.shape[0]
    devices = dec_n * tp_n
    z_n = dec_n // CORES
    x_n = 2 ** ((tp_n.bit_length()) // 2)
    y_n = tp_n // x_n
    half = width // HALVES
    dec, tp = lax.axis_index("dec"), lax.axis_index("tp")
    z, core = dec // CORES, dec % CORES
    y, x = tp // x_n, tp % x_n
    me = dec * tp_n + tp

    barrier = pltpu.get_barrier_semaphore()
    for d in range(1, dec_n):
        pl.semaphore_signal(barrier, inc=1, device_id=(flip(dec, d), tp), device_id_type=MESH)
    for d in range(1, tp_n):
        pl.semaphore_signal(barrier, inc=1, device_id=(dec, flip(tp, d)), device_id_type=MESH)
    load = pltpu.make_async_copy(lm_head, weights, w_sem)
    load.start()

    for s in range(slots):
        part = hidden[0, s]
        meansq = jnp.mean(part * part, axis=1, keepdims=True)
        fresh[s * length:(s + 1) * length, :] = part * lax.rsqrt(meansq + EPS) * gain[...]
    rows[me] = fresh[...].astype(jnp.bfloat16)

    lane = lax.broadcasted_iota(jnp.int32, (doc_ids.shape[1], 128), 1)
    slot = lax.broadcasted_iota(jnp.int32, (doc_ids.shape[1], 128), 0)
    values = ids[0].astype(jnp.float32)
    spread = jnp.zeros((doc_ids.shape[1], 128), jnp.float32)
    for l in range(length):
        spread = jnp.where(lane == slot * length + l, values[:, l:l + 1], spread)
    doc_ids[dec] = jnp.broadcast_to(jnp.sum(spread, axis=0, keepdims=True), spread.shape)
    stats[...] = jnp.zeros_like(stats)
    stat_doc[...] = jnp.zeros_like(stat_doc)

    pl.semaphore_wait(barrier, dec_n + tp_n - 2)

    def block(zz, cc, yy, xx):
        return (zz * CORES + cc) * tp_n + yy * x_n + xx

    def send(b, h, to_dec, to_tp):
        part = rows.at[b, :, pl.ds(h * half, half)]
        pltpu.make_async_remote_copy(
            src_ref=part, dst_ref=part, send_sem=send_sem, recv_sem=recv_sem.at[b, h],
            device_id=(to_dec, to_tp), device_id_type=MESH).start()

    def take(b, h):
        part = rows.at[b, :, pl.ds(h * half, half)]
        pltpu.make_async_copy(part, part, recv_sem.at[b, h]).wait()

    x_peers = [y * x_n + flip(x, d) for d in range(1, x_n)]
    y_peers = [flip(y, d) * x_n + x for d in range(1, y_n)]
    mate = flip(dec, 1)

    def send_x(b, h):
        for peer in x_peers:
            send(b, h, dec, peer)

    def send_y(b, h):
        for peer in y_peers:
            send(b, h, dec, peer)

    for h in range(HALVES):
        for d in range(1, z_n):
            send(me, h, flip(z, d) * CORES + core, tp)
        send_x(me, h)
        send_y(me, h)
        send(me, h, mate, tp)
        if h == 0:
            for d in range(1, dec_n):
                pltpu.make_async_remote_copy(
                    src_ref=doc_ids.at[dec], dst_ref=doc_ids.at[dec], send_sem=id_send,
                    recv_sem=id_recv, device_id=(flip(dec, d), tp), device_id_type=MESH).start()

    for h in range(HALVES):
        for d in range(z_n):
            zz = flip(z, d)
            if d:
                b = block(zz, core, y, x)
                take(b, h)
                send_x(b, h)
                send_y(b, h)
                send(b, h, mate, tp)
            for e in range(1, x_n):
                b = block(zz, core, y, flip(x, e))
                take(b, h)
                if h == 0:
                    send_y(b, h)
                send(b, h, mate, tp)
            for e in range(1, y_n):
                b = block(zz, core, flip(y, e), x)
                take(b, h)
                if h == 1:
                    send_x(b, h)
                send(b, h, mate, tp)
        for d in range(z_n):
            for e in range(1, x_n):
                for f in range(1, y_n):
                    b = block(flip(z, d), core, flip(y, f), flip(x, e))
                    take(b, h)
                    send(b, h, mate, tp)
    others = pltpu.make_async_copy(doc_ids.at[0:dec_n - 1], doc_ids.at[0:dec_n - 1], id_recv)
    others.wait()
    load.wait()
    for h in range(HALVES):
        for d in range(z_n):
            for e in range(x_n):
                for f in range(y_n):
                    take(block(flip(z, d), 1 - core, flip(y, f), flip(x, e)), h)

    for g in range(dec_n):
        id_row[0:1, g * doc_rows:(g + 1) * doc_rows] = doc_ids[g, 0:1, 0:doc_rows]

    total = devices * own_rows
    tile = min(256, total)
    blocks = tile // own_rows
    step = 512
    vocab_start = (dec * tp_n + tp) * vocab

    @pl.loop(0, total // tile)
    def _(t):
        logits[...] = jnp.zeros((vocab, tile), jnp.float32)

        @pl.loop(0, width // step)
        def _(k):
            at = pl.ds(pl.multiple_of(k * step, step), step)
            part = rows[pl.ds(t * blocks, blocks), :, at].astype(jnp.float32)
            part = part.reshape(tile, step).astype(jnp.bfloat16)
            logits[...] += lax.dot_general(
                weights[:, at], part, (((1,), (1,)), ((), ())),
                preferred_element_type=jnp.float32)

        value = logits[...]
        peak = jnp.max(value, axis=0, keepdims=True)
        place = pl.ds(pl.multiple_of(t * tile, tile), tile)
        entry = (lax.broadcasted_iota(jnp.int32, (vocab, tile), 0) + vocab_start).astype(jnp.float32)
        stat_row[0:1, place] = peak
        stat_row[1:2, place] = jnp.sum(jnp.exp(value - peak), axis=0, keepdims=True)
        stat_row[2:3, place] = jnp.sum(
            jnp.where(entry == id_row[0:1, place], value, 0.0), axis=0, keepdims=True)

    for g in range(dec_n):
        stats[g, 0:3, 0:doc_rows] = stat_row[0:3, g * doc_rows:(g + 1) * doc_rows]
    got_dec[dec] = stats[dec]
    for d in range(1, dec_n):
        to = flip(dec, d)
        pltpu.make_async_remote_copy(
            src_ref=stats.at[to], dst_ref=got_dec.at[dec], send_sem=dec_send,
            recv_sem=dec_recv, device_id=(to, tp), device_id_type=MESH).start()
    come = pltpu.make_async_copy(got_dec.at[0:dec_n - 1], got_dec.at[0:dec_n - 1], dec_recv)
    come.wait()

    def merged(got):
        peak = jnp.max(got[:, 0:1, :], axis=0)
        summed = jnp.sum(got[:, 1:2, :] * jnp.exp(got[:, 0:1, :] - peak[None]), axis=0)
        return peak, summed, jnp.sum(got[:, 2:3, :], axis=0)

    for i, value in enumerate(merged(got_dec[...])):
        stat_doc[i:i + 1, :] = value
    got_tp[tp] = stat_doc[...]
    for d in range(1, tp_n):
        pltpu.make_async_remote_copy(
            src_ref=stat_doc, dst_ref=got_tp.at[tp], send_sem=tp_send,
            recv_sem=tp_recv, device_id=(dec, flip(tp, d)), device_id_type=MESH).start()
    pltpu.make_async_copy(got_tp.at[0:tp_n - 1], got_tp.at[0:tp_n - 1], tp_recv).wait()
    peak, summed, target = merged(got_tp[...])

    logp = target - (peak + jnp.log(summed))
    score = logp
    for l in range(1, length):
        score = score + pltpu.roll(logp, 128 - l, 1)
    score = score / length
    lane = lax.broadcasted_iota(jnp.int32, (1, 128), 1)
    first = jnp.logical_and(lane % length == 0, lane < doc_rows)
    alive = jnp.logical_and(first, lane // length < counts[0])
    best = jnp.max(jnp.where(alive, score, -jnp.inf), axis=1, keepdims=True)
    norm = best + jnp.log(jnp.sum(
        jnp.exp(jnp.where(alive, score - best, -jnp.inf)), axis=1, keepdims=True))
    hyp = jnp.where(alive, score, 0.0)
    post = jnp.where(alive, score - norm, 0.0)
    out_lane = lax.broadcasted_iota(jnp.int32, (1, slots), 1)
    hyp_out = jnp.zeros((1, slots), jnp.float32)
    post_out = jnp.zeros((1, slots), jnp.float32)
    for s in range(slots):
        here = lane == (tp * slots + s) * length
        hyp_out = jnp.where(out_lane == s, jnp.sum(jnp.where(here, hyp, 0.0), axis=1, keepdims=True), hyp_out)
        post_out = jnp.where(out_lane == s, jnp.sum(jnp.where(here, post, 0.0), axis=1, keepdims=True), post_out)
    hyp_ref[...] = hyp_out
    post_ref[...] = post_out

    sent = rows.at[0:devices - 1]
    pltpu.make_async_copy(sent, sent, send_sem).wait()
    pltpu.make_async_copy(doc_ids.at[0:dec_n - 1], doc_ids.at[0:dec_n - 1], id_send).wait()
    pltpu.make_async_copy(got_dec.at[0:dec_n - 1], got_dec.at[0:dec_n - 1], dec_send).wait()
    pltpu.make_async_copy(got_tp.at[0:tp_n - 1], got_tp.at[0:tp_n - 1], tp_send).wait()


def body(dec_n, tp_n, hidden, norm_gain, lm_head, token_ids, doc_counts):
    slots, length, width = hidden.shape[1:]
    own_rows = slots * length
    devices = dec_n * tp_n
    vocab = lm_head.shape[0]
    total = devices * own_rows
    all_slots = token_ids.shape[1]
    vmem = pl.BlockSpec(memory_space=pltpu.VMEM)
    out = jax.ShapeDtypeStruct((1, slots), jnp.float32)
    dma = pltpu.SemaphoreType.DMA
    return pl.pallas_call(
        functools.partial(kernel, dec_n, tp_n),
        out_shape=(out, out),
        in_specs=[vmem, vmem, pl.BlockSpec(memory_space=pl.ANY), vmem,
                  pl.BlockSpec(memory_space=pltpu.SMEM)],
        out_specs=(vmem, vmem),
        scratch_shapes=[
            pltpu.VMEM((vocab, width), jnp.bfloat16),
            pltpu.VMEM((devices, own_rows, width), jnp.bfloat16),
            pltpu.VMEM((dec_n, all_slots, 128), jnp.float32),
            pltpu.VMEM((8, total), jnp.float32),
            pltpu.VMEM((own_rows, width), jnp.float32),
            pltpu.VMEM((vocab, min(256, total)), jnp.float32),
            pltpu.VMEM((8, total), jnp.float32),
            pltpu.VMEM((dec_n, 8, 128), jnp.float32),
            pltpu.VMEM((dec_n, 8, 128), jnp.float32),
            pltpu.VMEM((8, 128), jnp.float32),
            pltpu.VMEM((tp_n, 8, 128), jnp.float32),
            dma, dma, dma((devices, HALVES)), dma, dma, dma, dma, dma, dma,
        ],
        compiler_params=pltpu.CompilerParams(
            collective_id=0, has_side_effects=True, vmem_limit_bytes=48 * 1024 * 1024),
        name="rescore",
    )(hidden, norm_gain.reshape(1, width), lm_head, token_ids, doc_counts)


def solution(mesh):
    placed = (
        P("dec", "tp", None, None),
        P(),
        P(("dec", "tp"), None),
        P("dec", None, None),
        P("dec"),
    )
    return jax.shard_map(
        functools.partial(body, mesh.shape["dec"], mesh.shape["tp"]),
        mesh=mesh,
        in_specs=placed,
        out_specs=(P("dec", "tp"), P("dec", "tp")),
        check_vma=False,
    )
```

time: 147 us -> 52.9 us (0.36)
  blocking collectives: 107 us -> 0 us
  Pallas kernels: 0 us -> 45.7 us
  between operations: 17.4 us -> 1.29 us
  waiting for transfers between devices: 7.88 us -> 0 us
  other arithmetic: 4.67 us -> 0 us
  matrix products: 4.18 us -> 0 us
    pallas_call x0 -> x1, Pallas kernels: none -> 45.7 us  [body(): pl.pallas_call(functools.partial(kernel, dec_n, tp_n), out_shape=(out, ou...]
    pmax x1 -> x0, blocking collectives: 40.2 us -> none  [body(): global_peak = lax.pmax(peak_value, ('dec', 'tp'))]
    psum x1 -> x0, blocking collectives: 39 us -> none  [body(): sum_exp, target_sum = lax.psum((scaled, target), ('dec', 'tp'))]
    unnamed x2 -> x0, blocking collectives: 16.7 us -> none
    all_gather x1 -> x0, blocking collectives: 11.1 us -> none  [body(): lax.all_gather(normed, 'tp', axis=0, tiled=True)]
    all_gather x1 -> x0, waiting for transfers between devices: 7.87 us -> none  [body(): seg_rows = lax.all_gather(group_rows, 'dec', axis=0, tiled=True)]
    dot_general x1 -> x0, matrix products: 4.18 us -> none  [body(): lax.dot_general(seg_rows, lm_head, (((1,), (1,)), ((), ())), preferred_el...]
    reduce_sum x4 -> x0, other arithmetic: 2.69 us -> none  [the longest x1 1.25 us: body(): jnp.sum(jnp.exp(jnp.where(alive, block_scores - best_score, -jnp.inf)))]
  transfers between devices with their start and end apart: 1 -> 0, of which waited for: 1 -> 0; matrix products, arithmetic and copies ran while one was open for 2% -> 0% of each run, Pallas kernels for 0% -> 0%
where the time goes in v1:
time: 52.9 us; the launch traced here: 52.6 us
  Pallas kernels  45.7 us (86%)
  local copies, waits for them, and re-layouts  5.59 us (11%)
  between operations  1.29 us (2%)
    pallas_call x1, Pallas kernels, body(): pl.pallas_call(functools.partial(kernel, dec_n, tp_n), out_shape=(out, ou...  45.7 us
    unnamed x9, local copies, waits for them, and re-layouts  5.59 us

profile of v1, /device:TPU:0, one launch (start us, length us, event | category | flops | bytes accessed | tf_op | source)
XLA Modules:
  0.0 52.6 jit_solution(3127187343640391526)
XLA Ops:
  1.3 0.8 %copy.7.ids = s32[1,8,4]{2,1,0:T(8,128)S(1)} copy(s32[1,8,4]{1,2,0:T(4,128)} %param.8) | data formatting | bytes 256 | tf_op args[3]
  2.0 0.0 copy-start
  2.0 2.2 %copy-done = bf16[512,4096]{1,0:T(8,128)(2,1)S(1)} copy-done((bf16[512,4096]{1,0:T(8,128)(2,1)S(1)}, bf16[512,4096]{1,0:T(8,128)(2,1)}, u32[]{:S(2)}) %copy-start) | copy-done | bytes 4194328
  4.2 0.0 copy-start.1
  4.2 0.9 %copy-done.1 = f32[1,2,4,4096]{3,2,1,0:T(4,128)S(1)} copy-done((f32[1,2,4,4096]{3,2,1,0:T(4,128)S(1)}, f32[1,2,4,4096]{3,2,1,0:T(4,128)}, u32[]{:S(2)}) %copy-start.1) | copy-done | bytes 131096
  5.1 0.0 copy-start.2
  5.1 0.7 %copy-done.2 = f32[4096]{0:T(1024)S(1)} copy-done((f32[4096]{0:T(1024)S(1)}, f32[4096]{0:T(1024)}, u32[]{:S(2)}) %copy-start.2) | copy-done | bytes 16408
  5.8 45.7 %rescore.1 = (f32[1,2]{1,0:T(1,128)S(1)}, f32[1,2]{1,0:T(1,128)S(1)}) custom-call(f32[1,2,4,4096]{3,2,1,0:T(4,128)S(1)} %copy-done.1, f32[1,4096]{1,0:T(1,128)S(1)} %bitcast.1, bf16[512,4096]{1,0:T(8,128)(2,1)S(1)} %copy-done, s32[1,8,4]{2,1,0:T(8,128)S(1)} %copy.7.ids, s32[1]{0:T(128)S(6)} %copy.10.counts), custom_call_target="tpu_custom_call" | custom-call | tf_op jit(solution)/shard_map/rescore/pallas_call | solution.py:238
  51.6 0.5 copy.11
  52.1 0.5 copy.12
Async XLA Ops:
  2.0 2.2 %copy-start = (bf16[512,4096]{1,0:T(8,128)(2,1)S(1)}, bf16[512,4096]{1,0:T(8,128)(2,1)}, u32[]{:S(2)}) copy-start(bf16[512,4096]{1,0:T(8,128)(2,1)} %lm_head.1) | copy-start | bytes 12582916
  4.2 0.9 %copy-start.1 = (f32[1,2,4,4096]{3,2,1,0:T(4,128)S(1)}, f32[1,2,4,4096]{3,2,1,0:T(4,128)}, u32[]{:S(2)}) copy-start(f32[1,2,4,4096]{3,2,1,0:T(4,128)} %hidden.1) | copy-start | bytes 393220
  5.1 0.7 %copy-start.2 = (f32[4096]{0:T(1024)S(1)}, f32[4096]{0:T(1024)}, u32[]{:S(2)}) copy-start(f32[4096]{0:T(1024)} %param.6) | copy-start | bytes 49156

commit v2 on v1

--- a/solution.py
+++ b/solution.py
@@ -22,9 +22,9 @@
     return index
 
 
-def kernel(dec_n, tp_n, hidden, gain, lm_head, ids, counts, hyp_ref, post_ref,
-           weights, rows, doc_ids, id_row, fresh, logits, stat_row, stats, got_dec, stat_doc, got_tp,
-           w_sem, send_sem, recv_sem, id_send, id_recv, dec_send, dec_recv, tp_send, tp_recv):
+def kernel(dec_n, tp_n, hidden_hbm, gain_hbm, lm_head, ids_hbm, counts, hyp_ref, post_ref,
+           hidden, gain, ids, weights, rows, doc_ids, id_row, fresh, logits, stat_row, stats, got_dec, stat_doc, got_tp,
+           h_sem, g_sem, i_sem, w_sem, send_sem, recv_sem, id_send, id_recv, dec_send, dec_recv, tp_send, tp_recv):
     slots, length, width = hidden.shape[1:]
     own_rows = slots * length
     doc_rows = tp_n * own_rows
@@ -32,11 +32,13 @@
     devices = dec_n * tp_n
     z_n = dec_n // CORES
     x_n = 2 ** ((tp_n.bit_length()) // 2)
-    y_n = tp_n // x_n
+    assert x_n * x_n == tp_n
     half = width // HALVES
     dec, tp = lax.axis_index("dec"), lax.axis_index("tp")
     z, core = dec // CORES, dec % CORES
-    y, x = tp // x_n, tp % x_n
+    u_step = 1 + core * (x_n - 1)
+    v_step = x_n - core * (x_n - 1)
+    u, v = (tp // u_step) % x_n, (tp // v_step) % x_n
     me = dec * tp_n + tp
 
     barrier = pltpu.get_barrier_semaphore()
@@ -44,8 +46,12 @@
         pl.semaphore_signal(barrier, inc=1, device_id=(flip(dec, d), tp), device_id_type=MESH)
     for d in range(1, tp_n):
         pl.semaphore_signal(barrier, inc=1, device_id=(dec, flip(tp, d)), device_id_type=MESH)
-    load = pltpu.make_async_copy(lm_head, weights, w_sem)
-    load.start()
+    loads = [pltpu.make_async_copy(*pair) for pair in (
+        (hidden_hbm, hidden, h_sem), (gain_hbm, gain, g_sem), (ids_hbm, ids, i_sem), (lm_head, weights, w_sem))]
+    for load in loads:
+        load.start()
+    for load in loads[:3]:
+        load.wait()
 
     for s in range(slots):
         part = hidden[0, s]
@@ -53,90 +59,94 @@
         fresh[s * length:(s + 1) * length, :] = part * lax.rsqrt(meansq + EPS) * gain[...]
     rows[me] = fresh[...].astype(jnp.bfloat16)
 
-    lane = lax.broadcasted_iota(jnp.int32, (doc_ids.shape[1], 128), 1)
-    slot = lax.broadcasted_iota(jnp.int32, (doc_ids.shape[1], 128), 0)
+    all_slots = ids.shape[2]
+    lane = lax.broadcasted_iota(jnp.int32, (length, 128), 1)
+    token = lax.broadcasted_iota(jnp.int32, (length, 128), 0)
     values = ids[0].astype(jnp.float32)
-    spread = jnp.zeros((doc_ids.shape[1], 128), jnp.float32)
-    for l in range(length):
-        spread = jnp.where(lane == slot * length + l, values[:, l:l + 1], spread)
-    doc_ids[dec] = jnp.broadcast_to(jnp.sum(spread, axis=0, keepdims=True), spread.shape)
+    spread = jnp.zeros((length, 128), jnp.float32)
+    for s in range(all_slots):
+        spread = jnp.where(lane == s * length + token, values[:, s:s + 1], spread)
+    doc_ids[dec] = jnp.broadcast_to(jnp.sum(spread, axis=0, keepdims=True), doc_ids.shape[1:])
     stats[...] = jnp.zeros_like(stats)
     stat_doc[...] = jnp.zeros_like(stat_doc)
 
     pl.semaphore_wait(barrier, dec_n + tp_n - 2)
 
-    def block(zz, cc, yy, xx):
-        return (zz * CORES + cc) * tp_n + yy * x_n + xx
+    def block(zz, cc, vv, uu):
+        return (zz * CORES + cc) * tp_n + vv * v_step + uu * u_step
 
     def send(b, h, to_dec, to_tp):
         part = rows.at[b, :, pl.ds(h * half, half)]
         pltpu.make_async_remote_copy(
             src_ref=part, dst_ref=part, send_sem=send_sem, recv_sem=recv_sem.at[b, h],
             device_id=(to_dec, to_tp), device_id_type=MESH).start()
+
+    def send_mate(b):
+        pltpu.make_async_remote_copy(
+            src_ref=rows.at[b], dst_ref=rows.at[b], send_sem=send_sem, recv_sem=recv_sem.at[b, 0],
+            device_id=(flip(dec, 1), tp), device_id_type=MESH).start()
 
     def take(b, h):
         part = rows.at[b, :, pl.ds(h * half, half)]
         pltpu.make_async_copy(part, part, recv_sem.at[b, h]).wait()
 
-    x_peers = [y * x_n + flip(x, d) for d in range(1, x_n)]
-    y_peers = [flip(y, d) * x_n + x for d in range(1, y_n)]
-    mate = flip(dec, 1)
-
-    def send_x(b, h):
-        for peer in x_peers:
-            send(b, h, dec, peer)
-
-    def send_y(b, h):
-        for peer in y_peers:
-            send(b, h, dec, peer)
+    def send_u(b, h):
+        for d in range(1, x_n):
+            send(b, h, dec, v * v_step + flip(u, d) * u_step)
+
+    def send_v(b, h):
+        for d in range(1, x_n):
+            send(b, h, dec, flip(v, d) * v_step + u * u_step)
 
     for h in range(HALVES):
+        send_u(me, h)
         for d in range(1, z_n):
             send(me, h, flip(z, d) * CORES + core, tp)
-        send_x(me, h)
-        send_y(me, h)
-        send(me, h, mate, tp)
-        if h == 0:
-            for d in range(1, dec_n):
-                pltpu.make_async_remote_copy(
-                    src_ref=doc_ids.at[dec], dst_ref=doc_ids.at[dec], send_sem=id_send,
-                    recv_sem=id_recv, device_id=(flip(dec, d), tp), device_id_type=MESH).start()
+        send_v(me, h)
+    send_mate(me)
+    for d in range(1, dec_n):
+        pltpu.make_async_remote_copy(
+            src_ref=doc_ids.at[dec], dst_ref=doc_ids.at[dec], send_sem=id_send,
+            recv_sem=id_recv, device_id=(flip(dec, d), tp), device_id_type=MESH).start()
 
     for h in range(HALVES):
         for d in range(z_n):
             zz = flip(z, d)
             if d:
-                b = block(zz, core, y, x)
+                b = block(zz, core, v, u)
                 take(b, h)
-                send_x(b, h)
-                send_y(b, h)
-                send(b, h, mate, tp)
+                send_u(b, h)
+                send_v(b, h)
+                if h == 1:
+                    send_mate(b)
             for e in range(1, x_n):
-                b = block(zz, core, y, flip(x, e))
+                b = block(zz, core, v, flip(u, e))
                 take(b, h)
                 if h == 0:
-                    send_y(b, h)
-                send(b, h, mate, tp)
-            for e in range(1, y_n):
-                b = block(zz, core, flip(y, e), x)
+                    send_v(b, h)
+                else:
+                    send_mate(b)
+            for e in range(1, x_n):
+                b = block(zz, core, flip(v, e), u)
                 take(b, h)
                 if h == 1:
-                    send_x(b, h)
-                send(b, h, mate, tp)
-        for d in range(z_n):
-            for e in range(1, x_n):
-                for f in range(1, y_n):
-                    b = block(flip(z, d), core, flip(y, f), flip(x, e))
+                    send_u(b, h)
+                    send_mate(b)
+    for d in range(z_n):
+        for e in range(1, x_n):
+            for f in range(1, x_n):
+                b = block(flip(z, d), core, flip(v, f), flip(u, e))
+                for h in range(HALVES):
                     take(b, h)
-                    send(b, h, mate, tp)
+                send_mate(b)
     others = pltpu.make_async_copy(doc_ids.at[0:dec_n - 1], doc_ids.at[0:dec_n - 1], id_recv)
     others.wait()
-    load.wait()
-    for h in range(HALVES):
-        for d in range(z_n):
-            for e in range(x_n):
-                for f in range(y_n):
-                    take(block(flip(z, d), 1 - core, flip(y, f), flip(x, e)), h)
+    loads[3].wait()
+    for d in range(z_n):
+        for e in range(x_n):
+            for f in range(x_n):
+                b = block(flip(z, d), 1 - core, flip(v, f), flip(u, e))
+                pltpu.make_async_copy(rows.at[b], rows.at[b], recv_sem.at[b, 0]).wait()
 
     for g in range(dec_n):
         id_row[0:1, g * doc_rows:(g + 1) * doc_rows] = doc_ids[g, 0:1, 0:doc_rows]
@@ -238,13 +248,15 @@
     return pl.pallas_call(
         functools.partial(kernel, dec_n, tp_n),
         out_shape=(out, out),
-        in_specs=[vmem, vmem, pl.BlockSpec(memory_space=pl.ANY), vmem,
-                  pl.BlockSpec(memory_space=pltpu.SMEM)],
+        in_specs=[pl.BlockSpec(memory_space=pl.ANY)] * 4 + [pl.BlockSpec(memory_space=pltpu.SMEM)],
         out_specs=(vmem, vmem),
         scratch_shapes=[
+            pltpu.VMEM(hidden.shape, jnp.float32),
+            pltpu.VMEM((1, width), jnp.float32),
+            pltpu.VMEM((1, length, all_slots), jnp.int32),
             pltpu.VMEM((vocab, width), jnp.bfloat16),
             pltpu.VMEM((devices, own_rows, width), jnp.bfloat16),
-            pltpu.VMEM((dec_n, all_slots, 128), jnp.float32),
+            pltpu.VMEM((dec_n, 8, 128), jnp.float32),
             pltpu.VMEM((8, total), jnp.float32),
             pltpu.VMEM((own_rows, width), jnp.float32),
             pltpu.VMEM((vocab, min(256, total)), jnp.float32),
@@ -253,12 +265,12 @@
             pltpu.VMEM((dec_n, 8, 128), jnp.float32),
             pltpu.VMEM((8, 128), jnp.float32),
             pltpu.VMEM((tp_n, 8, 128), jnp.float32),
-            dma, dma, dma((devices, HALVES)), dma, dma, dma, dma, dma, dma,
+            dma, dma, dma, dma, dma, dma((devices, HALVES)), dma, dma, dma, dma, dma, dma,
         ],
         compiler_params=pltpu.CompilerParams(
-            collective_id=0, has_side_effects=True, vmem_limit_bytes=48 * 1024 * 1024),
+            collective_id=0, has_side_effects=True, vmem_limit_bytes=60 * 1024 * 1024),
         name="rescore",
-    )(hidden, norm_gain.reshape(1, width), lm_head, token_ids, doc_counts)
+    )(hidden, norm_gain.reshape(1, width), lm_head, jnp.swapaxes(token_ids, 1, 2), doc_counts)
 
 
 def solution(mesh):

time: 52.9 us -> 46.9 us (0.89)
  local copies, waits for them, and re-layouts: 5.59 us -> 2.25 us
  Pallas kernels: 45.7 us -> 43.2 us
    unnamed x9 -> x2, local copies, waits for them, and re-layouts: 5.59 us -> 2.25 us
    pallas_call x1, Pallas kernels: 45.7 us -> 43.2 us  [body(): pl.pallas_call(functools.partial(kernel, dec_n, tp_n), out_shape=(out, ou...]
where the time goes in v2:
time: 46.9 us; the launch traced here: 46.7 us
  Pallas kernels  43.2 us (92%)
  local copies, waits for them, and re-layouts  2.25 us (5%)
  between operations  1.29 us (3%)
    pallas_call x1, Pallas kernels, body(): pl.pallas_call(functools.partial(kernel, dec_n, tp_n), out_shape=(out, ou...  43.2 us
    unnamed x2, local copies, waits for them, and re-layouts  2.25 us

profile of v2, /device:TPU:0, one launch (start us, length us, event | category | flops | bytes accessed | tf_op | source)
XLA Modules:
  0.0 46.7 jit_solution(17189761876031432256)
XLA Ops:
  1.3 43.2 %rescore.1 = (f32[1,2]{1,0:T(1,128)}, f32[1,2]{1,0:T(1,128)}) custom-call(f32[1,2,4,4096]{3,2,1,0:T(4,128)} %hidden_hbm.1, f32[1,4096]{1,0:T(1,128)} %bitcast.2, bf16[512,4096]{1,0:T(8,128)(2,1)} %lm_head.1, s32[1,4,8]{2,1,0:T(4,128)} %bitcast.3, s32[1]{0:T(128)S(6)} %copy.9.counts), custom_call_target="tpu_custom_call" | custom-call | tf_op jit(solution)/shard_map/rescore/pallas_call | solution.py:248
  44.4 1.1 %copy.10 = f32[1,2]{1,0:T(1,128)} copy(f32[1,2]{1,0:T(1,128)} %get-tuple-element.4) | data formatting | bytes 16
  45.5 1.1 %copy.11 = f32[1,2]{1,0:T(1,128)} copy(f32[1,2]{1,0:T(1,128)} %get-tuple-element.5) | data formatting | bytes 16

commit v3 on v2

--- a/solution.py
+++ b/solution.py
@@ -22,13 +22,11 @@
     return index
 
 
-def kernel(dec_n, tp_n, hidden_hbm, gain_hbm, lm_head, ids_hbm, counts, hyp_ref, post_ref,
-           hidden, gain, ids, weights, rows, doc_ids, id_row, fresh, logits, stat_row, stats, got_dec, stat_doc, got_tp,
-           h_sem, g_sem, i_sem, w_sem, send_sem, recv_sem, id_send, id_recv, dec_send, dec_recv, tp_send, tp_recv):
+def gather_kernel(dec_n, tp_n, hidden_hbm, gain_hbm, ids_hbm, rows, doc_ids,
+                  hidden, gain, ids, fresh, h_sem, g_sem, i_sem, send_sem, recv_sem, id_send, id_recv):
     slots, length, width = hidden.shape[1:]
     own_rows = slots * length
     doc_rows = tp_n * own_rows
-    vocab = lm_head.shape[0]
     devices = dec_n * tp_n
     z_n = dec_n // CORES
     x_n = 2 ** ((tp_n.bit_length()) // 2)
@@ -47,10 +45,10 @@
     for d in range(1, tp_n):
         pl.semaphore_signal(barrier, inc=1, device_id=(dec, flip(tp, d)), device_id_type=MESH)
     loads = [pltpu.make_async_copy(*pair) for pair in (
-        (hidden_hbm, hidden, h_sem), (gain_hbm, gain, g_sem), (ids_hbm, ids, i_sem), (lm_head, weights, w_sem))]
+        (hidden_hbm, hidden, h_sem), (gain_hbm, gain, g_sem), (ids_hbm, ids, i_sem))]
     for load in loads:
         load.start()
-    for load in loads[:3]:
+    for load in loads:
         load.wait()
 
     for s in range(slots):
@@ -67,8 +65,6 @@
     for s in range(all_slots):
         spread = jnp.where(lane == s * length + token, values[:, s:s + 1], spread)
     doc_ids[dec] = jnp.broadcast_to(jnp.sum(spread, axis=0, keepdims=True), doc_ids.shape[1:])
-    stats[...] = jnp.zeros_like(stats)
-    stat_doc[...] = jnp.zeros_like(stat_doc)
 
     pl.semaphore_wait(barrier, dec_n + tp_n - 2)
 
@@ -141,46 +137,28 @@
                 send_mate(b)
     others = pltpu.make_async_copy(doc_ids.at[0:dec_n - 1], doc_ids.at[0:dec_n - 1], id_recv)
     others.wait()
-    loads[3].wait()
     for d in range(z_n):
         for e in range(x_n):
             for f in range(x_n):
                 b = block(flip(z, d), 1 - core, flip(v, f), flip(u, e))
                 pltpu.make_async_copy(rows.at[b], rows.at[b], recv_sem.at[b, 0]).wait()
 
-    for g in range(dec_n):
-        id_row[0:1, g * doc_rows:(g + 1) * doc_rows] = doc_ids[g, 0:1, 0:doc_rows]
-
-    total = devices * own_rows
-    tile = min(256, total)
-    blocks = tile // own_rows
-    step = 512
-    vocab_start = (dec * tp_n + tp) * vocab
-
-    @pl.loop(0, total // tile)
-    def _(t):
-        logits[...] = jnp.zeros((vocab, tile), jnp.float32)
-
-        @pl.loop(0, width // step)
-        def _(k):
-            at = pl.ds(pl.multiple_of(k * step, step), step)
-            part = rows[pl.ds(t * blocks, blocks), :, at].astype(jnp.float32)
-            part = part.reshape(tile, step).astype(jnp.bfloat16)
-            logits[...] += lax.dot_general(
-                weights[:, at], part, (((1,), (1,)), ((), ())),
-                preferred_element_type=jnp.float32)
-
-        value = logits[...]
-        peak = jnp.max(value, axis=0, keepdims=True)
-        place = pl.ds(pl.multiple_of(t * tile, tile), tile)
-        entry = (lax.broadcasted_iota(jnp.int32, (vocab, tile), 0) + vocab_start).astype(jnp.float32)
-        stat_row[0:1, place] = peak
-        stat_row[1:2, place] = jnp.sum(jnp.exp(value - peak), axis=0, keepdims=True)
-        stat_row[2:3, place] = jnp.sum(
-            jnp.where(entry == id_row[0:1, place], value, 0.0), axis=0, keepdims=True)
-
-    for g in range(dec_n):
-        stats[g, 0:3, 0:doc_rows] = stat_row[0:3, g * doc_rows:(g + 1) * doc_rows]
+    sent = rows.at[0:devices - 1]
+    pltpu.make_async_copy(sent, sent, send_sem).wait()
+    pltpu.make_async_copy(doc_ids.at[0:dec_n - 1], doc_ids.at[0:dec_n - 1], id_send).wait()
+
+
+def exchange_kernel(dec_n, tp_n, length, slots, stats, counts, hyp_ref, post_ref,
+                    got_dec, stat_doc, got_tp, dec_send, dec_recv, tp_send, tp_recv):
+    dec, tp = lax.axis_index("dec"), lax.axis_index("tp")
+    doc_rows = tp_n * slots * length
+    barrier = pltpu.get_barrier_semaphore()
+    for d in range(1, dec_n):
+        pl.semaphore_signal(barrier, inc=1, device_id=(flip(dec, d), tp), device_id_type=MESH)
+    for d in range(1, tp_n):
+        pl.semaphore_signal(barrier, inc=1, device_id=(dec, flip(tp, d)), device_id_type=MESH)
+    stat_doc[...] = jnp.zeros_like(stat_doc)
+    pl.semaphore_wait(barrier, dec_n + tp_n - 2)
     got_dec[dec] = stats[dec]
     for d in range(1, dec_n):
         to = flip(dec, d)
@@ -228,9 +206,6 @@
     hyp_ref[...] = hyp_out
     post_ref[...] = post_out
 
-    sent = rows.at[0:devices - 1]
-    pltpu.make_async_copy(sent, sent, send_sem).wait()
-    pltpu.make_async_copy(doc_ids.at[0:dec_n - 1], doc_ids.at[0:dec_n - 1], id_send).wait()
     pltpu.make_async_copy(got_dec.at[0:dec_n - 1], got_dec.at[0:dec_n - 1], dec_send).wait()
     pltpu.make_async_copy(got_tp.at[0:tp_n - 1], got_tp.at[0:tp_n - 1], tp_send).wait()
 
@@ -241,36 +216,53 @@
     devices = dec_n * tp_n
     vocab = lm_head.shape[0]
     total = devices * own_rows
+    doc_rows = total // dec_n
     all_slots = token_ids.shape[1]
     vmem = pl.BlockSpec(memory_space=pltpu.VMEM)
     out = jax.ShapeDtypeStruct((1, slots), jnp.float32)
     dma = pltpu.SemaphoreType.DMA
-    return pl.pallas_call(
-        functools.partial(kernel, dec_n, tp_n),
-        out_shape=(out, out),
-        in_specs=[pl.BlockSpec(memory_space=pl.ANY)] * 4 + [pl.BlockSpec(memory_space=pltpu.SMEM)],
+    rows, doc_ids = pl.pallas_call(
+        functools.partial(gather_kernel, dec_n, tp_n),
+        out_shape=(jax.ShapeDtypeStruct((devices, own_rows, width), jnp.bfloat16),
+                   jax.ShapeDtypeStruct((dec_n, 8, 128), jnp.float32)),
+        in_specs=[pl.BlockSpec(memory_space=pl.ANY)] * 3,
         out_specs=(vmem, vmem),
         scratch_shapes=[
             pltpu.VMEM(hidden.shape, jnp.float32),
             pltpu.VMEM((1, width), jnp.float32),
             pltpu.VMEM((1, length, all_slots), jnp.int32),
-            pltpu.VMEM((vocab, width), jnp.bfloat16),
-            pltpu.VMEM((devices, own_rows, width), jnp.bfloat16),
-            pltpu.VMEM((dec_n, 8, 128), jnp.float32),
-            pltpu.VMEM((8, total), jnp.float32),
             pltpu.VMEM((own_rows, width), jnp.float32),
-            pltpu.VMEM((vocab, min(256, total)), jnp.float32),
-            pltpu.VMEM((8, total), jnp.float32),
-            pltpu.VMEM((dec_n, 8, 128), jnp.float32),
+            dma, dma, dma, dma, dma((devices, HALVES)), dma, dma,
+        ],
+        compiler_params=pltpu.CompilerParams(
+            collective_id=0, has_side_effects=True, vmem_limit_bytes=40 * 1024 * 1024),
+        name="gather_rows",
+    )(hidden, norm_gain.reshape(1, width), jnp.swapaxes(token_ids, 1, 2))
+    logits = lax.dot_general(
+        lm_head, rows.reshape(total, width), (((1,), (1,)), ((), ())), preferred_element_type=jnp.float32)
+    vocab_start = (lax.axis_index("dec") * tp_n + lax.axis_index("tp")) * vocab
+    seg_ids = doc_ids[:, 0, :doc_rows].reshape(1, total)
+    peak = jnp.max(logits, axis=0, keepdims=True)
+    summed = jnp.sum(jnp.exp(logits - peak), axis=0, keepdims=True)
+    entry = (vocab_start + jnp.arange(vocab, dtype=jnp.int32)).astype(jnp.float32)
+    target = jnp.sum(jnp.where(entry[:, None] == seg_ids, logits, 0.0), axis=0, keepdims=True)
+    stats = jnp.concatenate([peak, summed, target], axis=0).reshape(3, dec_n, doc_rows)
+    stats = jnp.pad(jnp.swapaxes(stats, 0, 1), ((0, 0), (0, 5), (0, 128 - doc_rows)))
+    return pl.pallas_call(
+        functools.partial(exchange_kernel, dec_n, tp_n, length, slots),
+        out_shape=(out, out),
+        in_specs=[vmem, pl.BlockSpec(memory_space=pltpu.SMEM)],
+        out_specs=(vmem, vmem),
+        scratch_shapes=[
             pltpu.VMEM((dec_n, 8, 128), jnp.float32),
             pltpu.VMEM((8, 128), jnp.float32),
             pltpu.VMEM((tp_n, 8, 128), jnp.float32),
-            dma, dma, dma, dma, dma, dma((devices, HALVES)), dma, dma, dma, dma, dma, dma,
+            dma, dma, dma, dma,
         ],
         compiler_params=pltpu.CompilerParams(
-            collective_id=0, has_side_effects=True, vmem_limit_bytes=60 * 1024 * 1024),
-        name="rescore",
-    )(hidden, norm_gain.reshape(1, width), lm_head, jnp.swapaxes(token_ids, 1, 2), doc_counts)
+            collective_id=1, has_side_effects=True, vmem_limit_bytes=16 * 1024 * 1024),
+        name="exchange_parts",
+    )(stats, doc_counts)
 
 
 def solution(mesh):

time: 46.9 us -> 51.6 us (1.10)
  matrix products: 0 us -> 3.55 us
  local copies, waits for them, and re-layouts: 2.25 us -> 3.67 us
  Pallas kernels: 43.2 us -> 42.5 us
    dot_general x0 -> x1, matrix products: none -> 3.55 us  [body(): lax.dot_general(lm_head, rows.reshape(total, width), (((1,), (1,)), ((),...]
    unnamed x2 -> x8, local copies, waits for them, and re-layouts: 2.25 us -> 3.32 us
    pallas_call x1 -> x2, Pallas kernels: 43.2 us -> 42.5 us  [the longest x1 33.1 us: body(): pl.pallas_call(functools.partial(gather_kernel, dec_n, tp_n), out_shape=(...]
where the time goes in v3:
time: 51.6 us; the launch traced here: 51.3 us
  Pallas kernels  42.5 us (82%)
  local copies, waits for them, and re-layouts  3.67 us (7%)
  matrix products  3.55 us (7%)
  between operations  1.34 us (3%)
    pallas_call x1, Pallas kernels, body(): pl.pallas_call(functools.partial(gather_kernel, dec_n, tp_n), out_shape=(...  33.1 us
    pallas_call x1, Pallas kernels, body(): pl.pallas_call(functools.partial(exchange_kernel, dec_n, tp_n, length, sl...  9.36 us
    dot_general x1, matrix products, body(): lax.dot_general(lm_head, rows.reshape(total, width), (((1,), (1,)), ((),...  3.55 us
    unnamed x8, local copies, waits for them, and re-layouts  3.32 us

profile of v3, /device:TPU:0, one launch (start us, length us, event | category | flops | bytes accessed | tf_op | source)
XLA Modules:
  0.0 51.3 jit_solution(3325774771807718514)
XLA Ops:
  0.6 0.0 copy-start
  0.6 0.9 %copy-done = f32[1,2,4,4096]{3,2,1,0:T(4,128)S(1)} copy-done((f32[1,2,4,4096]{3,2,1,0:T(4,128)S(1)}, f32[1,2,4,4096]{3,2,1,0:T(4,128)}, u32[]{:S(2)}) %copy-start) | copy-done | bytes 131096
  1.5 0.0 copy-start.1
  1.5 0.7 %copy-done.1 = f32[4096]{0:T(1024)S(1)} copy-done((f32[4096]{0:T(1024)S(1)}, f32[4096]{0:T(1024)}, u32[]{:S(2)}) %copy-start.1) | copy-done | bytes 16408
  2.3 0.0 copy-start.2
  2.3 0.7 %copy-done.2 = s32[1,8,4]{1,2,0:T(4,128)S(1)} copy-done((s32[1,8,4]{1,2,0:T(4,128)S(1)}, s32[1,8,4]{1,2,0:T(4,128)}, u32[]{:S(2)}) %copy-start.2) | copy-done | bytes 152
  2.9 33.1 %gather_rows.1 = (bf16[32,8,4096]{2,1,0:T(8,128)(2,1)S(1)}, f32[8,8,128]{2,1,0:T(8,128)S(1)}) custom-call(f32[1,2,4,4096]{3,2,1,0:T(4,128)S(1)} %copy-done, f32[1,4096]{1,0:T(1,128)S(1)} %bitcast.19, s32[1,4,8]{2,1,0:T(4,128)S(1)} %bitcast.20), custom_call_target="tpu_custom_call" | custom-call | tf_op jit(solution)/shard_map/gather_rows/pallas_call | solution.py:224
  36.1 3.6 %fusion.5 = (f32[256]{0:T(256)S(1)}, f32[256,512]{1,0:T(8,128)S(1)}) fusion(bf16[512,4096]{1,0:T(8,128)(2,1)} %param.7, bf16[32,8,4096]{2,1,0:T(8,128)(2,1)S(1)} %get-tuple-element.4), kind=kOutput, calls=%fused_computation.10 | convolution fusion | flops 1073872640 | bytes 6816768 | tf_op jit(solution)/shard_map/dot_general | solution.py:241
  39.6 0.1 eq.16
  39.7 0.3 fusion.3
  40.0 0.1 concatenate.11
  40.1 0.1 concatenate.12
  40.2 0.1 concatenate.10
  41.0 9.4 %exchange_parts.1 = (f32[1,2]{1,0:T(1,128)S(1)}, f32[1,2]{1,0:T(1,128)S(1)}) custom-call(f32[8,8,128]{2,1,0:T(8,128)S(1)} %pad.4.stats, s32[1]{0:T(128)S(6)} %copy.9.counts), custom_call_target="tpu_custom_call" | custom-call | tf_op jit(solution)/shard_map/exchange_parts/pallas_call | solution.py:251
  50.3 0.5 copy.10
  50.8 0.5 copy.11
  (4 shorter events, 0.1 us)
Async XLA Ops:
  0.6 0.9 %copy-start = (f32[1,2,4,4096]{3,2,1,0:T(4,128)S(1)}, f32[1,2,4,4096]{3,2,1,0:T(4,128)}, u32[]{:S(2)}) copy-start(f32[1,2,4,4096]{3,2,1,0:T(4,128)} %hidden_hbm.1) | copy-start | bytes 393220
  1.5 0.7 %copy-start.1 = (f32[4096]{0:T(1024)S(1)}, f32[4096]{0:T(1024)}, u32[]{:S(2)}) copy-start(f32[4096]{0:T(1024)} %param.6) | copy-start | bytes 49156
  2.3 0.7 %copy-start.2 = (s32[1,8,4]{1,2,0:T(4,128)S(1)}, s32[1,8,4]{1,2,0:T(4,128)}, u32[]{:S(2)}) copy-start(s32[1,8,4]{1,2,0:T(4,128)} %param.8) | copy-start | bytes 388

commit v4 on v2

--- a/solution.py
+++ b/solution.py
@@ -24,22 +24,23 @@
 
 def kernel(dec_n, tp_n, hidden_hbm, gain_hbm, lm_head, ids_hbm, counts, hyp_ref, post_ref,
            hidden, gain, ids, weights, rows, doc_ids, id_row, fresh, logits, stat_row, stats, got_dec, stat_doc, got_tp,
-           h_sem, g_sem, i_sem, w_sem, send_sem, recv_sem, id_send, id_recv, dec_send, dec_recv, tp_send, tp_recv):
+           h_sem, g_sem, i_sem, w_sem, z_send, z_recv, u_send, u_recv, v_send, v_recv,
+           uv_send, uv_recv, vu_send, vu_recv, mate_send, mate_recv, id_send, id_recv, dec_send, dec_recv, tp_send, tp_recv):
     slots, length, width = hidden.shape[1:]
     own_rows = slots * length
     doc_rows = tp_n * own_rows
     vocab = lm_head.shape[0]
-    devices = dec_n * tp_n
     z_n = dec_n // CORES
     x_n = 2 ** ((tp_n.bit_length()) // 2)
     assert x_n * x_n == tp_n
     half = width // HALVES
+    piece_width = half // HALVES
+    z_half = z_n // 2
     dec, tp = lax.axis_index("dec"), lax.axis_index("tp")
     z, core = dec // CORES, dec % CORES
     u_step = 1 + core * (x_n - 1)
     v_step = x_n - core * (x_n - 1)
     u, v = (tp // u_step) % x_n, (tp // v_step) % x_n
-    me = dec * tp_n + tp
 
     barrier = pltpu.get_barrier_semaphore()
     for d in range(1, dec_n):
@@ -57,7 +58,8 @@
         part = hidden[0, s]
         meansq = jnp.mean(part * part, axis=1, keepdims=True)
         fresh[s * length:(s + 1) * length, :] = part * lax.rsqrt(meansq + EPS) * gain[...]
-    rows[me] = fresh[...].astype(jnp.bfloat16)
+    rows[z, core, tp] = jnp.concatenate(
+        [fresh[:, 0:half], fresh[:, half:width]], axis=0).astype(jnp.bfloat16)
 
     all_slots = ids.shape[2]
     lane = lax.broadcasted_iota(jnp.int32, (length, 128), 1)
@@ -72,103 +74,79 @@
 
     pl.semaphore_wait(barrier, dec_n + tp_n - 2)
 
-    def block(zz, cc, vv, uu):
-        return (zz * CORES + cc) * tp_n + vv * v_step + uu * u_step
-
-    def send(b, h, to_dec, to_tp):
-        part = rows.at[b, :, pl.ds(h * half, half)]
+    def place(vv, uu):
+        return vv * v_step + uu * u_step
+
+    def send(piece, send_sem, recv_sem, to_dec, to_tp):
         pltpu.make_async_remote_copy(
-            src_ref=part, dst_ref=part, send_sem=send_sem, recv_sem=recv_sem.at[b, h],
+            src_ref=piece, dst_ref=piece, send_sem=send_sem, recv_sem=recv_sem,
             device_id=(to_dec, to_tp), device_id_type=MESH).start()
 
-    def send_mate(b):
-        pltpu.make_async_remote_copy(
-            src_ref=rows.at[b], dst_ref=rows.at[b], send_sem=send_sem, recv_sem=recv_sem.at[b, 0],
-            device_id=(flip(dec, 1), tp), device_id_type=MESH).start()
-
-    def take(b, h):
-        part = rows.at[b, :, pl.ds(h * half, half)]
-        pltpu.make_async_copy(part, part, recv_sem.at[b, h]).wait()
-
-    def send_u(b, h):
-        for d in range(1, x_n):
-            send(b, h, dec, v * v_step + flip(u, d) * u_step)
-
-    def send_v(b, h):
-        for d in range(1, x_n):
-            send(b, h, dec, flip(v, d) * v_step + u * u_step)
-
-    for h in range(HALVES):
-        send_u(me, h)
-        for d in range(1, z_n):
-            send(me, h, flip(z, d) * CORES + core, tp)
-        send_v(me, h)
-    send_mate(me)
+    def wait(piece, sem):
+        pltpu.make_async_copy(piece, piece, sem).wait()
+
+    first_z = (z // z_half) * z_half
+    groups = [pl.ds(first_z, z_half), pl.ds(z_half - first_z, z_half)]
+    low, high = pl.ds(0, piece_width), pl.ds(piece_width, piece_width)
+    near = range(1, x_n)
+
+    for d in range(1, z_n):
+        send(rows.at[z, core, tp], z_send, z_recv.at[d // z_half], flip(z, d) * CORES + core, tp)
     for d in range(1, dec_n):
-        pltpu.make_async_remote_copy(
-            src_ref=doc_ids.at[dec], dst_ref=doc_ids.at[dec], send_sem=id_send,
-            recv_sem=id_recv, device_id=(flip(dec, d), tp), device_id_type=MESH).start()
-
-    for h in range(HALVES):
-        for d in range(z_n):
-            zz = flip(z, d)
-            if d:
-                b = block(zz, core, v, u)
-                take(b, h)
-                send_u(b, h)
-                send_v(b, h)
-                if h == 1:
-                    send_mate(b)
-            for e in range(1, x_n):
-                b = block(zz, core, v, flip(u, e))
-                take(b, h)
-                if h == 0:
-                    send_v(b, h)
-                else:
-                    send_mate(b)
-            for e in range(1, x_n):
-                b = block(zz, core, flip(v, e), u)
-                take(b, h)
-                if h == 1:
-                    send_u(b, h)
-                    send_mate(b)
-    for d in range(z_n):
-        for e in range(1, x_n):
-            for f in range(1, x_n):
-                b = block(flip(z, d), core, flip(v, f), flip(u, e))
-                for h in range(HALVES):
-                    take(b, h)
-                send_mate(b)
+        send(doc_ids.at[dec], id_send, id_recv, flip(dec, d), tp)
+    for g, group in enumerate(groups):
+        wait(rows.at[pl.ds(0, z_half - 1 + g), core, tp], z_recv.at[g])
+        column = rows.at[group, core, tp]
+        for e in near:
+            send(column, u_send, u_recv.at[g, e], dec, place(v, flip(u, e)))
+            send(column, v_send, v_recv.at[g, e], dec, place(flip(v, e), u))
+    for g, group in enumerate(groups):
+        for e in near:
+            at = place(v, flip(u, e))
+            wait(rows.at[group, core, at], u_recv.at[g, e])
+            for f in near:
+                send(rows.at[group, core, at, :, low], uv_send, uv_recv.at[g, e, f], dec, place(flip(v, f), u))
+            at = place(flip(v, e), u)
+            wait(rows.at[group, core, at], v_recv.at[g, e])
+            for f in near:
+                send(rows.at[group, core, at, :, high], vu_send, vu_recv.at[g, f, e], dec, place(v, flip(u, f)))
+    for g, group in enumerate(groups):
+        for e in near:
+            for f in near:
+                at = place(flip(v, f), flip(u, e))
+                wait(rows.at[group, core, at, :, low], uv_recv.at[g, e, f])
+                wait(rows.at[group, core, at, :, high], vu_recv.at[g, e, f])
+        send(rows.at[group, core], mate_send, mate_recv.at[g], flip(dec, 1), tp)
     others = pltpu.make_async_copy(doc_ids.at[0:dec_n - 1], doc_ids.at[0:dec_n - 1], id_recv)
     others.wait()
     loads[3].wait()
-    for d in range(z_n):
-        for e in range(x_n):
-            for f in range(x_n):
-                b = block(flip(z, d), 1 - core, flip(v, f), flip(u, e))
-                pltpu.make_async_copy(rows.at[b], rows.at[b], recv_sem.at[b, 0]).wait()
+    for g, group in enumerate(groups):
+        wait(rows.at[group, 1 - core], mate_recv.at[g])
 
     for g in range(dec_n):
         id_row[0:1, g * doc_rows:(g + 1) * doc_rows] = doc_ids[g, 0:1, 0:doc_rows]
 
-    total = devices * own_rows
-    tile = min(256, total)
-    blocks = tile // own_rows
+    total = dec_n * doc_rows
+    decs = max(1, min(256, total) // doc_rows)
+    tile = decs * doc_rows
     step = 512
+    flat = rows.reshape(dec_n, tp_n, HALVES * own_rows, half)
     vocab_start = (dec * tp_n + tp) * vocab
 
     @pl.loop(0, total // tile)
     def _(t):
         logits[...] = jnp.zeros((vocab, tile), jnp.float32)
 
-        @pl.loop(0, width // step)
+        @pl.loop(0, half // step)
         def _(k):
             at = pl.ds(pl.multiple_of(k * step, step), step)
-            part = rows[pl.ds(t * blocks, blocks), :, at].astype(jnp.float32)
-            part = part.reshape(tile, step).astype(jnp.bfloat16)
-            logits[...] += lax.dot_general(
-                weights[:, at], part, (((1,), (1,)), ((), ())),
-                preferred_element_type=jnp.float32)
+            beyond = pl.ds(pl.multiple_of(k * step + half, step), step)
+            both = flat[pl.ds(t * decs, decs), :, :, at].astype(jnp.float32)
+            for side, columns in enumerate((at, beyond)):
+                some = both[:, :, side * own_rows:(side + 1) * own_rows].reshape(tile, step)
+                logits[...] += lax.dot_general(
+                    weights[:, columns], some.astype(jnp.bfloat16), (((1,), (1,)), ((), ())),
+                    preferred_element_type=jnp.float32)
 
         value = logits[...]
         peak = jnp.max(value, axis=0, keepdims=True)
@@ -228,8 +206,12 @@
     hyp_ref[...] = hyp_out
     post_ref[...] = post_out
 
-    sent = rows.at[0:devices - 1]
-    pltpu.make_async_copy(sent, sent, send_sem).wait()
+    wait(rows.at[0:z_n - 1, 0, 0], z_send)
+    for sem in (u_send, v_send):
+        wait(rows.at[:, 0, 0:x_n - 1], sem)
+    for sem in (uv_send, vu_send):
+        wait(rows.at[:, 0, 0:(x_n - 1) ** 2, :, low], sem)
+    wait(rows.at[:, 0], mate_send)
     pltpu.make_async_copy(doc_ids.at[0:dec_n - 1], doc_ids.at[0:dec_n - 1], id_send).wait()
     pltpu.make_async_copy(got_dec.at[0:dec_n - 1], got_dec.at[0:dec_n - 1], dec_send).wait()
     pltpu.make_async_copy(got_tp.at[0:tp_n - 1], got_tp.at[0:tp_n - 1], tp_send).wait()
@@ -245,6 +227,7 @@
     vmem = pl.BlockSpec(memory_space=pltpu.VMEM)
     out = jax.ShapeDtypeStruct((1, slots), jnp.float32)
     dma = pltpu.SemaphoreType.DMA
+    side = 2 ** (tp_n.bit_length() // 2)
     return pl.pallas_call(
         functools.partial(kernel, dec_n, tp_n),
         out_shape=(out, out),
@@ -255,7 +238,7 @@
             pltpu.VMEM((1, width), jnp.float32),
             pltpu.VMEM((1, length, all_slots), jnp.int32),
             pltpu.VMEM((vocab, width), jnp.bfloat16),
-            pltpu.VMEM((devices, own_rows, width), jnp.bfloat16),
+            pltpu.VMEM((dec_n // CORES, CORES, tp_n, HALVES * own_rows, width // HALVES), jnp.bfloat16),
             pltpu.VMEM((dec_n, 8, 128), jnp.float32),
             pltpu.VMEM((8, total), jnp.float32),
             pltpu.VMEM((own_rows, width), jnp.float32),
@@ -265,7 +248,9 @@
             pltpu.VMEM((dec_n, 8, 128), jnp.float32),
             pltpu.VMEM((8, 128), jnp.float32),
             pltpu.VMEM((tp_n, 8, 128), jnp.float32),
-            dma, dma, dma, dma, dma, dma((devices, HALVES)), dma, dma, dma, dma, dma, dma,
+            dma, dma, dma, dma, dma, dma((2,)), dma, dma((2, side)), dma, dma((2, side)),
+            dma, dma((2, side, side)), dma, dma((2, side, side)), dma, dma((2,)),
+            dma, dma, dma, dma, dma, dma,
         ],
         compiler_params=pltpu.CompilerParams(
             collective_id=0, has_side_effects=True, vmem_limit_bytes=60 * 1024 * 1024),

time: 46.9 us -> 37.5 us (0.80)
  Pallas kernels: 43.2 us -> 33.8 us
    pallas_call x1, Pallas kernels: 43.2 us -> 33.8 us  [body(): pl.pallas_call(functools.partial(kernel, dec_n, tp_n), out_shape=(out, ou...]
where the time goes in v4:
time: 37.5 us; the launch traced here: 37.3 us
  Pallas kernels  33.8 us (90%)
  local copies, waits for them, and re-layouts  2.25 us (6%)
  between operations  1.29 us (3%)
    pallas_call x1, Pallas kernels, body(): pl.pallas_call(functools.partial(kernel, dec_n, tp_n), out_shape=(out, ou...  33.8 us
    unnamed x2, local copies, waits for them, and re-layouts  2.25 us

profile of v4, /device:TPU:0, one launch (start us, length us, event | category | flops | bytes accessed | tf_op | source)
XLA Modules:
  0.0 37.3 jit_solution(15028411715121220951)
XLA Ops:
  1.3 33.8 %rescore.1 = (f32[1,2]{1,0:T(1,128)}, f32[1,2]{1,0:T(1,128)}) custom-call(f32[1,2,4,4096]{3,2,1,0:T(4,128)} %hidden_hbm.1, f32[1,4096]{1,0:T(1,128)} %bitcast.2, bf16[512,4096]{1,0:T(8,128)(2,1)} %lm_head.1, s32[1,4,8]{2,1,0:T(4,128)} %bitcast.3, s32[1]{0:T(128)S(6)} %copy.9.counts), custom_call_target="tpu_custom_call" | custom-call | tf_op jit(solution)/shard_map/rescore/pallas_call | solution.py:231
  35.0 1.1 %copy.10 = f32[1,2]{1,0:T(1,128)} copy(f32[1,2]{1,0:T(1,128)} %get-tuple-element.4) | data formatting | bytes 16
  36.1 1.1 %copy.11 = f32[1,2]{1,0:T(1,128)} copy(f32[1,2]{1,0:T(1,128)} %get-tuple-element.5) | data formatting | bytes 16

commit v5 on v4

--- a/solution.py
+++ b/solution.py
@@ -10,6 +10,7 @@
 MESH = pl.DeviceIdType.MESH
 CORES = 2
 HALVES = 2
+ID_LANES = 128
 EPS = 1e-05
 
 
@@ -23,9 +24,9 @@
 
 
 def kernel(dec_n, tp_n, hidden_hbm, gain_hbm, lm_head, ids_hbm, counts, hyp_ref, post_ref,
-           hidden, gain, ids, weights, rows, doc_ids, id_row, fresh, logits, stat_row, stats, got_dec, stat_doc, got_tp,
+           hidden, gain, ids, weights, rows, fresh, logits, stats, got_dec, stat_doc, got_tp,
            h_sem, g_sem, i_sem, w_sem, z_send, z_recv, u_send, u_recv, v_send, v_recv,
-           uv_send, uv_recv, vu_send, vu_recv, mate_send, mate_recv, id_send, id_recv, dec_send, dec_recv, tp_send, tp_recv):
+           uv_send, uv_recv, vu_send, vu_recv, mate_send, mate_recv, dec_send, dec_recv, tp_send, tp_recv):
     slots, length, width = hidden.shape[1:]
     own_rows = slots * length
     doc_rows = tp_n * own_rows
@@ -58,17 +59,20 @@
         part = hidden[0, s]
         meansq = jnp.mean(part * part, axis=1, keepdims=True)
         fresh[s * length:(s + 1) * length, :] = part * lax.rsqrt(meansq + EPS) * gain[...]
-    rows[z, core, tp] = jnp.concatenate(
+    rows[z, core, tp, :, 0:half] = jnp.concatenate(
         [fresh[:, 0:half], fresh[:, half:width]], axis=0).astype(jnp.bfloat16)
 
-    all_slots = ids.shape[2]
-    lane = lax.broadcasted_iota(jnp.int32, (length, 128), 1)
-    token = lax.broadcasted_iota(jnp.int32, (length, 128), 0)
-    values = ids[0].astype(jnp.float32)
-    spread = jnp.zeros((length, 128), jnp.float32)
-    for s in range(all_slots):
-        spread = jnp.where(lane == s * length + token, values[:, s:s + 1], spread)
-    doc_ids[dec] = jnp.broadcast_to(jnp.sum(spread, axis=0, keepdims=True), doc_ids.shape[1:])
+    lane = lax.broadcasted_iota(jnp.int32, (length, ID_LANES), 1)
+    slot = lax.broadcasted_iota(jnp.int32, ids.shape[1:], 1)
+    digits = []
+    for s in range(slots):
+        here = jnp.where(slot == tp * slots + s, ids[0], 0).astype(jnp.float32)
+        token = jnp.sum(here, axis=1, keepdims=True).astype(jnp.int32)
+        shift = jnp.where(lane == 0, 12, jnp.where(lane == 1, 6, 0))
+        digit = jnp.bitwise_and(jnp.right_shift(jnp.broadcast_to(token, lane.shape), shift), 63)
+        digits.append(jnp.where(lane < 3, digit, 0).astype(jnp.float32))
+    digits.append(jnp.zeros((own_rows, ID_LANES), jnp.float32))
+    rows[z, core, tp, :, half:half + ID_LANES] = jnp.concatenate(digits, axis=0).astype(jnp.bfloat16)
     stats[...] = jnp.zeros_like(stats)
     stat_doc[...] = jnp.zeros_like(stat_doc)
 
@@ -87,13 +91,11 @@
 
     first_z = (z // z_half) * z_half
     groups = [pl.ds(first_z, z_half), pl.ds(z_half - first_z, z_half)]
-    low, high = pl.ds(0, piece_width), pl.ds(piece_width, piece_width)
+    low, high = pl.ds(0, piece_width), pl.ds(piece_width, piece_width + ID_LANES)
     near = range(1, x_n)
 
     for d in range(1, z_n):
         send(rows.at[z, core, tp], z_send, z_recv.at[d // z_half], flip(z, d) * CORES + core, tp)
-    for d in range(1, dec_n):
-        send(doc_ids.at[dec], id_send, id_recv, flip(dec, d), tp)
     for g, group in enumerate(groups):
         wait(rows.at[pl.ds(0, z_half - 1 + g), core, tp], z_recv.at[g])
         column = rows.at[group, core, tp]
@@ -117,48 +119,49 @@
                 wait(rows.at[group, core, at, :, low], uv_recv.at[g, e, f])
                 wait(rows.at[group, core, at, :, high], vu_recv.at[g, e, f])
         send(rows.at[group, core], mate_send, mate_recv.at[g], flip(dec, 1), tp)
-    others = pltpu.make_async_copy(doc_ids.at[0:dec_n - 1], doc_ids.at[0:dec_n - 1], id_recv)
-    others.wait()
     loads[3].wait()
+
+    z_some = max(1, min(256, z_n * doc_rows) // doc_rows)
+    tile = z_some * doc_rows
+    step = 512
+    vocab_start = (dec * tp_n + tp) * vocab
+    column = lax.broadcasted_iota(jnp.int32, (8, ID_LANES), 1)
+    scale = jnp.where(column == 0, 4096.0, jnp.where(column == 1, 64.0, jnp.where(column == 2, 1.0, 0.0)))
+
+    def times_rows(left, right):
+        return lax.dot_general(left, right.reshape(tile, right.shape[-1]).astype(jnp.bfloat16),
+                               (((1,), (1,)), ((), ())), preferred_element_type=jnp.float32)
+
+    def score_rows(which):
+        @pl.loop(0, z_n // z_some)
+        def _(t):
+            logits[...] = jnp.zeros((vocab, tile), jnp.float32)
+            some = pl.ds(t * z_some, z_some)
+
+            @pl.loop(0, half // step)
+            def _(k):
+                at = pl.ds(pl.multiple_of(k * step, step), step)
+                beyond = pl.ds(pl.multiple_of(k * step + half, step), step)
+                both = rows[some, which, :, :, at].astype(jnp.float32)
+                logits[...] += (times_rows(weights[:, at], both[:, :, 0:own_rows])
+                                + times_rows(weights[:, beyond], both[:, :, own_rows:2 * own_rows]))
+
+            tail = rows[some, which, :, :, pl.ds(half, ID_LANES)].astype(jnp.float32)
+            row_ids = times_rows(scale.astype(jnp.bfloat16), tail[:, :, 0:own_rows])[0:1, :]
+            value = logits[...]
+            peak = jnp.max(value, axis=0, keepdims=True)
+            summed = jnp.sum(jnp.exp(value - peak), axis=0, keepdims=True)
+            entry = (lax.broadcasted_iota(jnp.int32, (vocab, tile), 0) + vocab_start).astype(jnp.float32)
+            target = jnp.sum(jnp.where(entry == row_ids, value, 0.0), axis=0, keepdims=True)
+            for i in range(z_some):
+                for j, stat in enumerate((peak, summed, target)):
+                    stats[(t * z_some + i) * CORES + which, j:j + 1, 0:doc_rows] = stat[:, i * doc_rows:(i + 1) * doc_rows]
+
+    score_rows(core)
     for g, group in enumerate(groups):
         wait(rows.at[group, 1 - core], mate_recv.at[g])
-
-    for g in range(dec_n):
-        id_row[0:1, g * doc_rows:(g + 1) * doc_rows] = doc_ids[g, 0:1, 0:doc_rows]
-
-    total = dec_n * doc_rows
-    decs = max(1, min(256, total) // doc_rows)
-    tile = decs * doc_rows
-    step = 512
-    flat = rows.reshape(dec_n, tp_n, HALVES * own_rows, half)
-    vocab_start = (dec * tp_n + tp) * vocab
-
-    @pl.loop(0, total // tile)
-    def _(t):
-        logits[...] = jnp.zeros((vocab, tile), jnp.float32)
-
-        @pl.loop(0, half // step)
-        def _(k):
-            at = pl.ds(pl.multiple_of(k * step, step), step)
-            beyond = pl.ds(pl.multiple_of(k * step + half, step), step)
-            both = flat[pl.ds(t * decs, decs), :, :, at].astype(jnp.float32)
-            for side, columns in enumerate((at, beyond)):
-                some = both[:, :, side * own_rows:(side + 1) * own_rows].reshape(tile, step)
-                logits[...] += lax.dot_general(
-                    weights[:, columns], some.astype(jnp.bfloat16), (((1,), (1,)), ((), ())),
-                    preferred_element_type=jnp.float32)
-
-        value = logits[...]
-        peak = jnp.max(value, axis=0, keepdims=True)
-        place = pl.ds(pl.multiple_of(t * tile, tile), tile)
-        entry = (lax.broadcasted_iota(jnp.int32, (vocab, tile), 0) + vocab_start).astype(jnp.float32)
-        stat_row[0:1, place] = peak
-        stat_row[1:2, place] = jnp.sum(jnp.exp(value - peak), axis=0, keepdims=True)
-        stat_row[2:3, place] = jnp.sum(
-            jnp.where(entry == id_row[0:1, place], value, 0.0), axis=0, keepdims=True)
-
-    for g in range(dec_n):
-        stats[g, 0:3, 0:doc_rows] = stat_row[0:3, g * doc_rows:(g + 1) * doc_rows]
+    score_rows(1 - core)
+
     got_dec[dec] = stats[dec]
     for d in range(1, dec_n):
         to = flip(dec, d)
@@ -209,10 +212,9 @@
     wait(rows.at[0:z_n - 1, 0, 0], z_send)
     for sem in (u_send, v_send):
         wait(rows.at[:, 0, 0:x_n - 1], sem)
-    for sem in (uv_send, vu_send):
-        wait(rows.at[:, 0, 0:(x_n - 1) ** 2, :, low], sem)
+    for sem, piece in ((uv_send, low), (vu_send, high)):
+        wait(rows.at[:, 0, 0:(x_n - 1) ** 2, :, piece], sem)
     wait(rows.at[:, 0], mate_send)
-    pltpu.make_async_copy(doc_ids.at[0:dec_n - 1], doc_ids.at[0:dec_n - 1], id_send).wait()
     pltpu.make_async_copy(got_dec.at[0:dec_n - 1], got_dec.at[0:dec_n - 1], dec_send).wait()
     pltpu.make_async_copy(got_tp.at[0:tp_n - 1], got_tp.at[0:tp_n - 1], tp_send).wait()
 
@@ -220,9 +222,9 @@
 def body(dec_n, tp_n, hidden, norm_gain, lm_head, token_ids, doc_counts):
     slots, length, width = hidden.shape[1:]
     own_rows = slots * length
-    devices = dec_n * tp_n
     vocab = lm_head.shape[0]
-    total = devices * own_rows
+    doc_rows = tp_n * own_rows
+    z_some = max(1, min(256, dec_n // CORES * doc_rows) // doc_rows)
     all_slots = token_ids.shape[1]
     vmem = pl.BlockSpec(memory_space=pltpu.VMEM)
     out = jax.ShapeDtypeStruct((1, slots), jnp.float32)
@@ -238,19 +240,16 @@
             pltpu.VMEM((1, width), jnp.float32),
             pltpu.VMEM((1, length, all_slots), jnp.int32),
             pltpu.VMEM((vocab, width), jnp.bfloat16),
-            pltpu.VMEM((dec_n // CORES, CORES, tp_n, HALVES * own_rows, width // HALVES), jnp.bfloat16),
-            pltpu.VMEM((dec_n, 8, 128), jnp.float32),
-            pltpu.VMEM((8, total), jnp.float32),
+            pltpu.VMEM((dec_n // CORES, CORES, tp_n, HALVES * own_rows, width // HALVES + ID_LANES), jnp.bfloat16),
             pltpu.VMEM((own_rows, width), jnp.float32),
-            pltpu.VMEM((vocab, min(256, total)), jnp.float32),
-            pltpu.VMEM((8, total), jnp.float32),
+            pltpu.VMEM((vocab, z_some * doc_rows), jnp.float32),
             pltpu.VMEM((dec_n, 8, 128), jnp.float32),
             pltpu.VMEM((dec_n, 8, 128), jnp.float32),
             pltpu.VMEM((8, 128), jnp.float32),
             pltpu.VMEM((tp_n, 8, 128), jnp.float32),
             dma, dma, dma, dma, dma, dma((2,)), dma, dma((2, side)), dma, dma((2, side)),
             dma, dma((2, side, side)), dma, dma((2, side, side)), dma, dma((2,)),
-            dma, dma, dma, dma, dma, dma,
+            dma, dma, dma, dma,
         ],
         compiler_params=pltpu.CompilerParams(
             collective_id=0, has_side_effects=True, vmem_limit_bytes=60 * 1024 * 1024),

time: 37.5 us -> 38.3 us (1.021)
  Pallas kernels: 33.8 us -> 34.6 us
    pallas_call x1, Pallas kernels: 33.8 us -> 34.6 us  [body(): pl.pallas_call(functools.partial(kernel, dec_n, tp_n), out_shape=(out, ou...]
where the time goes in v5:
time: 38.3 us; the launch traced here: 38.1 us
  Pallas kernels  34.6 us (90%)
  local copies, waits for them, and re-layouts  2.25 us (6%)
  between operations  1.29 us (3%)
    pallas_call x1, Pallas kernels, body(): pl.pallas_call(functools.partial(kernel, dec_n, tp_n), out_shape=(out, ou...  34.6 us
    unnamed x2, local copies, waits for them, and re-layouts  2.25 us

profile of v5, /device:TPU:0, one launch (start us, length us, event | category | flops | bytes accessed | tf_op | source)
XLA Modules:
  0.0 38.1 jit_solution(14190211098231890466)
XLA Ops:
  1.3 34.6 %rescore.1 = (f32[1,2]{1,0:T(1,128)}, f32[1,2]{1,0:T(1,128)}) custom-call(f32[1,2,4,4096]{3,2,1,0:T(4,128)} %hidden_hbm.1, f32[1,4096]{1,0:T(1,128)} %bitcast.2, bf16[512,4096]{1,0:T(8,128)(2,1)} %lm_head.1, s32[1,4,8]{2,1,0:T(4,128)} %bitcast.3, s32[1]{0:T(128)S(6)} %copy.9.counts), custom_call_target="tpu_custom_call" | custom-call | tf_op jit(solution)/shard_map/rescore/pallas_call | solution.py:233
  35.9 1.1 %copy.10 = f32[1,2]{1,0:T(1,128)} copy(f32[1,2]{1,0:T(1,128)} %get-tuple-element.4) | data formatting | bytes 16
  37.0 1.1 %copy.11 = f32[1,2]{1,0:T(1,128)} copy(f32[1,2]{1,0:T(1,128)} %get-tuple-element.5) | data formatting | bytes 16

commit v6 on v5

--- a/solution.py
+++ b/solution.py
@@ -43,15 +43,15 @@
     v_step = x_n - core * (x_n - 1)
     u, v = (tp // u_step) % x_n, (tp // v_step) % x_n
 
+    loads = [pltpu.make_async_copy(*pair) for pair in (
+        (hidden_hbm, hidden, h_sem), (gain_hbm, gain, g_sem), (ids_hbm, ids, i_sem), (lm_head, weights, w_sem))]
+    for load in loads:
+        load.start()
     barrier = pltpu.get_barrier_semaphore()
     for d in range(1, dec_n):
         pl.semaphore_signal(barrier, inc=1, device_id=(flip(dec, d), tp), device_id_type=MESH)
     for d in range(1, tp_n):
         pl.semaphore_signal(barrier, inc=1, device_id=(dec, flip(tp, d)), device_id_type=MESH)
-    loads = [pltpu.make_async_copy(*pair) for pair in (
-        (hidden_hbm, hidden, h_sem), (gain_hbm, gain, g_sem), (ids_hbm, ids, i_sem), (lm_head, weights, w_sem))]
-    for load in loads:
-        load.start()
     for load in loads[:3]:
         load.wait()
 
@@ -121,9 +121,10 @@
         send(rows.at[group, core], mate_send, mate_recv.at[g], flip(dec, 1), tp)
     loads[3].wait()
 
-    z_some = max(1, min(256, z_n * doc_rows) // doc_rows)
-    tile = z_some * doc_rows
-    step = 512
+    decs = max(1, min(256, dec_n * doc_rows) // doc_rows)
+    tile = decs * doc_rows
+    step = 1024
+    flat = rows.reshape(dec_n, tp_n, 2 * own_rows, half + ID_LANES)
     vocab_start = (dec * tp_n + tp) * vocab
     column = lax.broadcasted_iota(jnp.int32, (8, ID_LANES), 1)
     scale = jnp.where(column == 0, 4096.0, jnp.where(column == 1, 64.0, jnp.where(column == 2, 1.0, 0.0)))
@@ -132,35 +133,33 @@
         return lax.dot_general(left, right.reshape(tile, right.shape[-1]).astype(jnp.bfloat16),
                                (((1,), (1,)), ((), ())), preferred_element_type=jnp.float32)
 
-    def score_rows(which):
-        @pl.loop(0, z_n // z_some)
-        def _(t):
-            logits[...] = jnp.zeros((vocab, tile), jnp.float32)
-            some = pl.ds(t * z_some, z_some)
-
-            @pl.loop(0, half // step)
-            def _(k):
-                at = pl.ds(pl.multiple_of(k * step, step), step)
-                beyond = pl.ds(pl.multiple_of(k * step + half, step), step)
-                both = rows[some, which, :, :, at].astype(jnp.float32)
-                logits[...] += (times_rows(weights[:, at], both[:, :, 0:own_rows])
-                                + times_rows(weights[:, beyond], both[:, :, own_rows:2 * own_rows]))
-
-            tail = rows[some, which, :, :, pl.ds(half, ID_LANES)].astype(jnp.float32)
-            row_ids = times_rows(scale.astype(jnp.bfloat16), tail[:, :, 0:own_rows])[0:1, :]
-            value = logits[...]
-            peak = jnp.max(value, axis=0, keepdims=True)
-            summed = jnp.sum(jnp.exp(value - peak), axis=0, keepdims=True)
-            entry = (lax.broadcasted_iota(jnp.int32, (vocab, tile), 0) + vocab_start).astype(jnp.float32)
-            target = jnp.sum(jnp.where(entry == row_ids, value, 0.0), axis=0, keepdims=True)
-            for i in range(z_some):
-                for j, stat in enumerate((peak, summed, target)):
-                    stats[(t * z_some + i) * CORES + which, j:j + 1, 0:doc_rows] = stat[:, i * doc_rows:(i + 1) * doc_rows]
-
-    score_rows(core)
     for g, group in enumerate(groups):
         wait(rows.at[group, 1 - core], mate_recv.at[g])
-    score_rows(1 - core)
+
+    @pl.loop(0, dec_n // decs)
+    def _(t):
+        logits[...] = jnp.zeros((vocab, tile), jnp.float32)
+        some = pl.ds(t * decs, decs)
+
+        @pl.loop(0, half // step)
+        def _(k):
+            at = pl.ds(pl.multiple_of(k * step, step), step)
+            beyond = pl.ds(pl.multiple_of(k * step + half, step), step)
+            both = flat[some, :, :, at].astype(jnp.float32)
+            logits[...] += (times_rows(weights[:, at], both[:, :, 0:own_rows])
+                            + times_rows(weights[:, beyond], both[:, :, own_rows:2 * own_rows]))
+
+        tail = flat[some, :, :, pl.ds(half, ID_LANES)].astype(jnp.float32)
+        row_ids = times_rows(scale.astype(jnp.bfloat16), tail[:, :, 0:own_rows])[0:1, :]
+        value = logits[...]
+        peak = jnp.max(value, axis=0, keepdims=True)
+        summed = jnp.sum(jnp.exp(value - peak), axis=0, keepdims=True)
+        entry = (lax.broadcasted_iota(jnp.int32, (vocab, tile), 0) + vocab_start).astype(jnp.float32)
+        target = jnp.sum(jnp.where(entry == row_ids, value, 0.0), axis=0, keepdims=True)
+        which = lax.broadcasted_iota(jnp.int32, (8, tile), 0)
+        stat = jnp.where(which == 0, peak, jnp.where(which == 1, summed, target))
+        for i in range(decs):
+            stats[t * decs + i, :, 0:doc_rows] = stat[:, i * doc_rows:(i + 1) * doc_rows]
 
     got_dec[dec] = stats[dec]
     for d in range(1, dec_n):
@@ -224,7 +223,7 @@
     own_rows = slots * length
     vocab = lm_head.shape[0]
     doc_rows = tp_n * own_rows
-    z_some = max(1, min(256, dec_n // CORES * doc_rows) // doc_rows)
+    decs = max(1, min(256, dec_n * doc_rows) // doc_rows)
     all_slots = token_ids.shape[1]
     vmem = pl.BlockSpec(memory_space=pltpu.VMEM)
     out = jax.ShapeDtypeStruct((1, slots), jnp.float32)
@@ -242,7 +241,7 @@
             pltpu.VMEM((vocab, width), jnp.bfloat16),
             pltpu.VMEM((dec_n // CORES, CORES, tp_n, HALVES * own_rows, width // HALVES + ID_LANES), jnp.bfloat16),
             pltpu.VMEM((own_rows, width), jnp.float32),
-            pltpu.VMEM((vocab, z_some * doc_rows), jnp.float32),
+            pltpu.VMEM((vocab, decs * doc_rows), jnp.float32),
             pltpu.VMEM((dec_n, 8, 128), jnp.float32),
             pltpu.VMEM((dec_n, 8, 128), jnp.float32),
             pltpu.VMEM((8, 128), jnp.float32),

time: 38.3 us -> 37.4 us (0.977)
  Pallas kernels: 34.6 us -> 33.7 us
    pallas_call x1, Pallas kernels: 34.6 us -> 33.7 us  [body(): pl.pallas_call(functools.partial(kernel, dec_n, tp_n), out_shape=(out, ou...]
where the time goes in v6:
time: 37.4 us; the launch traced here: 37.2 us
  Pallas kernels  33.7 us (90%)
  local copies, waits for them, and re-layouts  2.25 us (6%)
  between operations  1.29 us (3%)
    pallas_call x1, Pallas kernels, body(): pl.pallas_call(functools.partial(kernel, dec_n, tp_n), out_shape=(out, ou...  33.7 us
    unnamed x2, local copies, waits for them, and re-layouts  2.25 us

profile of v6, /device:TPU:0, one launch (start us, length us, event | category | flops | bytes accessed | tf_op | source)
XLA Modules:
  0.0 37.2 jit_solution(6526251468652472109)
XLA Ops:
  1.3 33.7 %rescore.1 = (f32[1,2]{1,0:T(1,128)}, f32[1,2]{1,0:T(1,128)}) custom-call(f32[1,2,4,4096]{3,2,1,0:T(4,128)} %hidden_hbm.1, f32[1,4096]{1,0:T(1,128)} %bitcast.2, bf16[512,4096]{1,0:T(8,128)(2,1)} %lm_head.1, s32[1,4,8]{2,1,0:T(4,128)} %bitcast.3, s32[1]{0:T(128)S(6)} %copy.9.counts), custom_call_target="tpu_custom_call" | custom-call | tf_op jit(solution)/shard_map/rescore/pallas_call | solution.py:232
  35.0 1.1 %copy.10 = f32[1,2]{1,0:T(1,128)} copy(f32[1,2]{1,0:T(1,128)} %get-tuple-element.4) | data formatting | bytes 16
  36.1 1.1 %copy.11 = f32[1,2]{1,0:T(1,128)} copy(f32[1,2]{1,0:T(1,128)} %get-tuple-element.5) | data formatting | bytes 16

commit v7 on v6

--- a/solution.py
+++ b/solution.py
@@ -96,29 +96,42 @@
 
     for d in range(1, z_n):
         send(rows.at[z, core, tp], z_send, z_recv.at[d // z_half], flip(z, d) * CORES + core, tp)
+    def send_near(piece, g):
+        for e in near:
+            send(piece, u_send, u_recv.at[g, e], dec, place(v, flip(u, e)))
+            send(piece, v_send, v_recv.at[g, e], dec, place(flip(v, e), u))
+
+    def send_mate(piece, g):
+        send(piece, mate_send, mate_recv.at[g], flip(dec, 1), tp)
+
+    send_near(rows.at[z, core, tp], 0)
     for g, group in enumerate(groups):
         wait(rows.at[pl.ds(0, z_half - 1 + g), core, tp], z_recv.at[g])
-        column = rows.at[group, core, tp]
-        for e in near:
-            send(column, u_send, u_recv.at[g, e], dec, place(v, flip(u, e)))
-            send(column, v_send, v_recv.at[g, e], dec, place(flip(v, e), u))
+        if g == 0:
+            for d in range(1, z_half):
+                send_near(rows.at[flip(z, d), core, tp], g)
+        else:
+            send_near(rows.at[group, core, tp], g)
+        send_mate(rows.at[group, core, tp], g)
     for g, group in enumerate(groups):
         for e in near:
             at = place(v, flip(u, e))
             wait(rows.at[group, core, at], u_recv.at[g, e])
             for f in near:
                 send(rows.at[group, core, at, :, low], uv_send, uv_recv.at[g, e, f], dec, place(flip(v, f), u))
+            send_mate(rows.at[group, core, at], g)
             at = place(flip(v, e), u)
             wait(rows.at[group, core, at], v_recv.at[g, e])
             for f in near:
                 send(rows.at[group, core, at, :, high], vu_send, vu_recv.at[g, f, e], dec, place(v, flip(u, f)))
+            send_mate(rows.at[group, core, at], g)
     for g, group in enumerate(groups):
         for e in near:
             for f in near:
                 at = place(flip(v, f), flip(u, e))
                 wait(rows.at[group, core, at, :, low], uv_recv.at[g, e, f])
                 wait(rows.at[group, core, at, :, high], vu_recv.at[g, e, f])
-        send(rows.at[group, core], mate_send, mate_recv.at[g], flip(dec, 1), tp)
+                send_mate(rows.at[group, core, at], g)
     loads[3].wait()
 
     decs = max(1, min(256, dec_n * doc_rows) // doc_rows)

time: 37.4 us -> 36.8 us (0.984)
  Pallas kernels: 33.7 us -> 33.1 us
    pallas_call x1, Pallas kernels: 33.7 us -> 33.1 us  [body(): pl.pallas_call(functools.partial(kernel, dec_n, tp_n), out_shape=(out, ou...]
where the time goes in v7:
time: 36.8 us; the launch traced here: 36.6 us
  Pallas kernels  33.1 us (90%)
  local copies, waits for them, and re-layouts  2.25 us (6%)
  between operations  1.29 us (4%)
    pallas_call x1, Pallas kernels, body(): pl.pallas_call(functools.partial(kernel, dec_n, tp_n), out_shape=(out, ou...  33.1 us
    unnamed x2, local copies, waits for them, and re-layouts  2.25 us

profile of v7, /device:TPU:0, one launch (start us, length us, event | category | flops | bytes accessed | tf_op | source)
XLA Modules:
  0.0 36.6 jit_solution(7246917119426452745)
XLA Ops:
  1.3 33.1 %rescore.1 = (f32[1,2]{1,0:T(1,128)}, f32[1,2]{1,0:T(1,128)}) custom-call(f32[1,2,4,4096]{3,2,1,0:T(4,128)} %hidden_hbm.1, f32[1,4096]{1,0:T(1,128)} %bitcast.2, bf16[512,4096]{1,0:T(8,128)(2,1)} %lm_head.1, s32[1,4,8]{2,1,0:T(4,128)} %bitcast.3, s32[1]{0:T(128)S(6)} %copy.9.counts), custom_call_target="tpu_custom_call" | custom-call | tf_op jit(solution)/shard_map/rescore/pallas_call | solution.py:245
  34.4 1.1 %copy.10 = f32[1,2]{1,0:T(1,128)} copy(f32[1,2]{1,0:T(1,128)} %get-tuple-element.4) | data formatting | bytes 16
  35.5 1.1 %copy.11 = f32[1,2]{1,0:T(1,128)} copy(f32[1,2]{1,0:T(1,128)} %get-tuple-element.5) | data formatting | bytes 16

commit v8 on v7

--- a/solution.py
+++ b/solution.py
@@ -23,7 +23,7 @@
     return index
 
 
-def kernel(dec_n, tp_n, hidden_hbm, gain_hbm, lm_head, ids_hbm, counts, hyp_ref, post_ref,
+def kernel(dec_n, tp_n, hidden_hbm, gain_hbm, lm_head, ids_hbm, counts, out_ref,
            hidden, gain, ids, weights, rows, fresh, logits, stats, got_dec, stat_doc, got_tp,
            h_sem, g_sem, i_sem, w_sem, z_send, z_recv, u_send, u_recv, v_send, v_recv,
            uv_send, uv_recv, vu_send, vu_recv, mate_send, mate_recv, dec_send, dec_recv, tp_send, tp_recv):
@@ -218,8 +218,8 @@
         here = lane == (tp * slots + s) * length
         hyp_out = jnp.where(out_lane == s, jnp.sum(jnp.where(here, hyp, 0.0), axis=1, keepdims=True), hyp_out)
         post_out = jnp.where(out_lane == s, jnp.sum(jnp.where(here, post, 0.0), axis=1, keepdims=True), post_out)
-    hyp_ref[...] = hyp_out
-    post_ref[...] = post_out
+    out_ref[0:1, :] = hyp_out
+    out_ref[1:2, :] = post_out
 
     wait(rows.at[0:z_n - 1, 0, 0], z_send)
     for sem in (u_send, v_send):
@@ -239,14 +239,14 @@
     decs = max(1, min(256, dec_n * doc_rows) // doc_rows)
     all_slots = token_ids.shape[1]
     vmem = pl.BlockSpec(memory_space=pltpu.VMEM)
-    out = jax.ShapeDtypeStruct((1, slots), jnp.float32)
+    out = jax.ShapeDtypeStruct((2, slots), jnp.float32)
     dma = pltpu.SemaphoreType.DMA
     side = 2 ** (tp_n.bit_length() // 2)
-    return pl.pallas_call(
+    scores = pl.pallas_call(
         functools.partial(kernel, dec_n, tp_n),
-        out_shape=(out, out),
+        out_shape=out,
         in_specs=[pl.BlockSpec(memory_space=pl.ANY)] * 4 + [pl.BlockSpec(memory_space=pltpu.SMEM)],
-        out_specs=(vmem, vmem),
+        out_specs=vmem,
         scratch_shapes=[
             pltpu.VMEM(hidden.shape, jnp.float32),
             pltpu.VMEM((1, width), jnp.float32),
@@ -267,6 +267,7 @@
             collective_id=0, has_side_effects=True, vmem_limit_bytes=60 * 1024 * 1024),
         name="rescore",
     )(hidden, norm_gain.reshape(1, width), lm_head, jnp.swapaxes(token_ids, 1, 2), doc_counts)
+    return scores[0:1], scores[1:2]
 
 
 def solution(mesh):

time: 36.8 us -> 35.9 us (0.976)
  local copies, waits for them, and re-layouts: 2.25 us -> 1.25 us
    unnamed x2 -> x0, local copies, waits for them, and re-layouts: 2.25 us -> none
    slice x0 -> x1, local copies, waits for them, and re-layouts: none -> 1.25 us  [body(): return (scores[0:1], scores[1:2])]
where the time goes in v8:
time: 35.9 us; the launch traced here: 35.7 us
  Pallas kernels  33.1 us (92%)
  between operations  1.29 us (4%)
  local copies, waits for them, and re-layouts  1.25 us (3%)
    pallas_call x1, Pallas kernels, body(): pl.pallas_call(functools.partial(kernel, dec_n, tp_n), out_shape=out, in_...  33.1 us
    slice x1, local copies, waits for them, and re-layouts, body(): return (scores[0:1], scores[1:2])  1.25 us

profile of v8, /device:TPU:0, one launch (start us, length us, event | category | flops | bytes accessed | tf_op | source)
XLA Modules:
  0.0 35.7 jit_solution(7690230320784789523)
XLA Ops:
  1.3 33.1 %rescore.1 = f32[2,2]{1,0:T(2,128)} custom-call(f32[1,2,4,4096]{3,2,1,0:T(4,128)} %hidden_hbm.1, f32[1,4096]{1,0:T(1,128)} %bitcast.2, bf16[512,4096]{1,0:T(8,128)(2,1)} %lm_head.1, s32[1,4,8]{2,1,0:T(4,128)} %bitcast.3, s32[1]{0:T(128)S(6)} %copy.7.counts), custom_call_target="tpu_custom_call" | custom-call | tf_op jit(solution)/shard_map/rescore/pallas_call | solution.py:245
  34.4 1.3 %fusion = (f32[1,2]{1,0:T(1,128)}, f32[1,2]{1,0:T(1,128)}) fusion(f32[2,2]{1,0:T(2,128)} %rescore.1), kind=kLoop, calls=%fused_computation | loop fusion | bytes 32 | tf_op jit(solution)/shard_map/slice | solution.py:270
